TPU v7x, 32 devices: a whole 2x2x4 slice. The times are simulated.
32 devices in a mesh: ctx: 16 (over z, y, x), tp: 2 (over core).
Axes of the slice: x: 2, y: 2, z: 4, core: 2. Of those that a mesh axis runs over, the one named last changes fastest.
Arguments:
- lin_query: bfloat16 [2048, 4096], P('ctx', 'tp'), may hold values from -6 to 6
- lin_key: bfloat16 [2048, 4096], P('ctx', 'tp'), may hold values from -6 to 6
- lin_value: bfloat16 [2048, 4096], P('ctx', 'tp'), may hold values from -6 to 6
- lin_cotangent: bfloat16 [2048, 4096], P('ctx', 'tp'), may hold values from -6 to 6
- soft_query: bfloat16 [2048, 4096], P('ctx', 'tp'), may hold values from -200 to 200
- soft_key: bfloat16 [2048, 1024], P('ctx', 'tp'), may hold values from -200 to 200
- soft_value: bfloat16 [2048, 1024], P('ctx', 'tp'), may hold values from -6 to 6
- doc_start: int32 [2048], P('ctx'), may hold values from 0 to 2047, as said below
Outputs:
- lin_out: bfloat16 [2048, 4096], P('ctx', 'tp')
- grad_query: bfloat16 [2048, 4096], P('ctx', 'tp')
- grad_key: bfloat16 [2048, 4096], P('ctx', 'tp')
- grad_value: bfloat16 [2048, 4096], P('ctx', 'tp')
- soft_out: bfloat16 [2048, 4096], P('ctx', 'tp')
Inputs may be any that keep to these rules, and one draw needn't show every extreme that they name: doc_start[i] <= i, doc_start never falls along the sequence, doc_start[0] = 0, doc_start[i] equals i or doc_start[i - 1], and a document of one position starts at position 2047.
All inputs are finite; a program needn't handle non-finite values.
Results may differ from a plain program's by a relative error of at most 0.011.
Values may be sent and summed in bfloat16 or wider, within the bound.
A program may use at most 128 MiB of HBM per device.

v0:
```python
import math

import jax
import jax.numpy as jnp
from jax import lax
from jax.sharding import PartitionSpec as P

HD = 128
LH = 32
SH = 32
KVH = 8


epsilon = 1e-06
highest = lax.Precision.HIGHEST
floor_score = -1e30


def carried_in(value, axis, combine, identity, reverse):
    length, position = (lax.axis_size(axis), lax.axis_index(axis))
    everything = lax.all_gather(value.astype(jnp.bfloat16), axis)
    start = jnp.broadcast_to(jnp.asarray(identity, value.dtype), value.shape)

    def hop(k, before):
        at = length - 1 - k if reverse else k
        reached = at > position if reverse else at < position
        new = combine(before, everything[at].astype(value.dtype))
        return jnp.where(reached, new, before)

    return lax.fori_loop(0, length, hop, start)


def on_device(
    lin_query, lin_key, lin_value, lin_cotangent, soft_query, soft_key, soft_value, doc_start
):
    length = lin_query.shape[0]
    heads_here = lin_query.shape[1] // HD
    queries = lin_query.reshape(length, heads_here, HD)
    keys = lin_key.reshape(length, heads_here, HD)
    values = lin_value.reshape(length, heads_here, HD)
    lower = jnp.tril(jnp.ones((length, length), dtype=bool))
    raw_scores = jnp.einsum("thd,shd->hts", queries, keys, preferred_element_type=jnp.float32)
    weights = jnp.where(lower[None], raw_scores, 0.0).astype(jnp.bfloat16)
    own_state = jnp.einsum("thd,the->hde", keys, values, preferred_element_type=jnp.float32)
    earlier = carried_in(own_state, "ctx", jnp.add, jnp.zeros_like(own_state), False)
    mixed = jnp.einsum("hts,shd->thd", weights, values, preferred_element_type=jnp.float32)
    mixed = mixed + jnp.einsum(
        "thd,hde->the", queries.astype(jnp.float32), earlier, precision=highest
    )
    mixed = mixed.reshape(length, heads_here * HD)
    squares = lax.psum(jnp.sum(mixed * mixed, axis=1), "tp")
    scale = lax.rsqrt(squares / (LH * HD) + epsilon)
    normed = mixed * scale[:, None]
    lin_out = normed.astype(jnp.bfloat16)
    grad = lin_cotangent.astype(jnp.float32)
    inner = lax.psum(jnp.sum(grad * normed, axis=1), "tp")
    grad_mix = scale[:, None] * (grad - normed * (inner / (LH * HD))[:, None])
    grad_mix = grad_mix.astype(jnp.bfloat16).reshape(length, heads_here, HD)
    own_adjoint = jnp.einsum("thd,the->hde", queries, grad_mix, preferred_element_type=jnp.float32)
    later = carried_in(own_adjoint, "ctx", jnp.add, jnp.zeros_like(own_adjoint), True)
    raw_grad = jnp.einsum("the,she->hts", grad_mix, values, preferred_element_type=jnp.float32)
    grad_scores = jnp.where(lower[None], raw_grad, 0.0).astype(jnp.bfloat16)
    grad_q = jnp.einsum("hts,shd->thd", grad_scores, keys, preferred_element_type=jnp.float32)
    grad_q = grad_q + jnp.einsum(
        "the,hde->thd", grad_mix.astype(jnp.float32), earlier, precision=highest
    )
    grad_k = jnp.einsum("hts,thd->shd", grad_scores, queries, preferred_element_type=jnp.float32)
    grad_k = grad_k + jnp.einsum(
        "she,hde->shd", values.astype(jnp.float32), later, precision=highest
    )
    grad_v = jnp.einsum("hts,thd->shd", weights, grad_mix, preferred_element_type=jnp.float32)
    grad_v = grad_v + jnp.einsum("shd,hde->she", keys.astype(jnp.float32), later, precision=highest)
    grad_query = grad_q.reshape(length, heads_here * HD).astype(jnp.bfloat16)
    grad_key = grad_k.reshape(length, heads_here * HD).astype(jnp.bfloat16)
    grad_value = grad_v.reshape(length, heads_here * HD).astype(jnp.bfloat16)
    group = SH // KVH
    kv_here = soft_key.shape[1] // HD
    factor = 1.0 / math.sqrt(HD)
    soft_q = soft_query.reshape(length, kv_here, group, HD)
    my_first = lax.axis_index("ctx") * length
    query_pos = my_first + jnp.arange(length, dtype=jnp.int32)

    def attend(carry, key_rows, value_rows, start):
        count = key_rows.shape[0]
        key_pos = start + jnp.arange(count, dtype=jnp.int32)
        allowed = (key_pos[None, :] <= query_pos[:, None]) & (
            key_pos[None, :] >= doc_start[:, None]
        )
        key_heads = key_rows.reshape(count, kv_here, HD)
        value_heads = value_rows.reshape(count, kv_here, HD)
        scores = (
            jnp.einsum("tkgd,nkd->kgtn", soft_q, key_heads, preferred_element_type=jnp.float32)
            * factor
        )
        scores = jnp.where(allowed, scores, floor_score)
        old_top, old_total, old_acc = carry
        new_top = jnp.maximum(old_top, jnp.max(scores, axis=-1))
        probs = jnp.where(allowed, jnp.exp(scores - new_top[..., None]), 0.0)
        shrink = jnp.exp(old_top - new_top)
        new_total = shrink * old_total + jnp.sum(probs, axis=-1)
        update = jnp.einsum(
            "kgtn,nkd->kgtd",
            probs.astype(jnp.bfloat16),
            value_heads,
            preferred_element_type=jnp.float32,
        )
        return (new_top, new_total, shrink[..., None] * old_acc + update)

    def visit(carry, key_rows, value_rows, start):
        return attend(carry, key_rows, value_rows, start)

    initial = (
        jnp.full((kv_here, group, length), floor_score, jnp.float32),
        jnp.zeros((kv_here, group, length), jnp.float32),
        jnp.zeros((kv_here, group, length, HD), jnp.float32),
    )
    key_rows = lax.all_gather(soft_key, "ctx", axis=0, tiled=True)
    value_rows = lax.all_gather(soft_value, "ctx", axis=0, tiled=True)
    count = key_rows.shape[0]
    block = math.gcd(count, 512)

    def inner_step(index, state):
        key_part = lax.dynamic_slice_in_dim(key_rows, index * block, block, 0)
        value_part = lax.dynamic_slice_in_dim(value_rows, index * block, block, 0)
        return visit(state, key_part, value_part, index * block)

    final = lax.fori_loop(0, count // block, inner_step, initial)
    top, total, accum = final
    result = accum / total[..., None]
    soft_out = (
        jnp.transpose(result, (2, 0, 1, 3))
        .reshape(length, kv_here * group * HD)
        .astype(jnp.bfloat16)
    )
    return (lin_out, grad_query, grad_key, grad_value, soft_out)


def solution(mesh):
    placed = (
        P("ctx", "tp"),
        P("ctx", "tp"),
        P("ctx", "tp"),
        P("ctx", "tp"),
        P("ctx", "tp"),
        P("ctx", "tp"),
        P("ctx", "tp"),
        P("ctx"),
    )
    return jax.shard_map(
        on_device,
        mesh=mesh,
        in_specs=placed,
        out_specs=(P("ctx", "tp"), P("ctx", "tp"), P("ctx", "tp"), P("ctx", "tp"), P("ctx", "tp")),
        check_vma=False,
    )
```

profile of v0, /device:TPU:0, one launch (start us, length us, event | category | flops | bytes accessed | tf_op | source)
XLA Modules:
  0.0 412.4 jit_solution(15832933753119914703)
XLA Ops:
  12.5 114.5 %all-gather.11.cloned.1.call-done = bf16[256,128,128]{2,1,0:T(8,128)(2,1)} async-done(((bf16[16,128,128]{2,1,0:T(8,128)(2,1)}), bf16[256,128,128]{2,1,0:T(8,128)(2,1)}) %all-gather.11.cloned.1.call-update) | async-done | bytes 8388624 | tf_op jit(solution)/shard_map/all_gather | solution.py:21
  127.0 26.2 %while.48 = (s32[]{:T(128)}, f32[16,128,128]{2,1,0:T(8,128)S(1)}, s32[]{:T(128)}, bf16[16,16,128,128]{3,2,1,0:T(8,128)(2,1)}, s32[]{:T(128)}, /*index=5*/s32[]{:T(128)}) while((s32[]{:T(128)}, f32[16,128,128]{2,1,0:T(8,128)S(1)}, s32[]{:T(128)}, bf16[16,16,128,128]{3,2,1,0:T(8,128)(2,1)}, s32[]{:T(128)}, ...), condition=%wide.region_1.2_spmd.clone, body=%wide.region_0.1_spmd.clone.sunk | while | flops 1048580 | bytes 2621533 | solution.py:30
  157.2 2.5 psum.14
  161.0 2.6 psum.15
  163.7 2.3 fusion.26
  168.7 2.1 copy.93
  172.1 19.6 %all-gather.7.cloned.1.call-done = bf16[2048,512]{0,1:T(8,128)(2,1)} async-done(((bf16[128,512]{0,1:T(8,128)(2,1)}), bf16[2048,512]{0,1:T(8,128)(2,1)}) %all-gather.7.cloned.1.call-update) | async-done | bytes 2097168 | tf_op jit(solution)/shard_map/all_gather | solution.py:117
  191.7 64.2 %all-gather.9.cloned.1.call-done = bf16[2048,512]{0,1:T(8,128)(2,1)} async-done(((bf16[128,512]{0,1:T(8,128)(2,1)}), bf16[2048,512]{0,1:T(8,128)(2,1)}) %all-gather.9.cloned.1.call-update) | async-done | bytes 2097168 | tf_op jit(solution)/shard_map/all_gather | solution.py:118
  255.9 49.5 %while.50 = (s32[]{:T(128)}, f32[4,4,128]{2,1,0:T(4,128)S(1)}, f32[4,4,128]{2,1,0:T(4,128)S(1)}, f32[4,4,128,128]{3,2,1,0:T(8,128)}, s32[128]{0:T(128)S(1)}, /*i...) while((s32[]{:T(128)}, f32[4,4,128]{2,1,0:T(4,128)S(1)}, ...), condition=%wide.region_11.12_spmd.clone, body=%wide.region_8.11_spmd.clone.sunk | while | flops 551496320 | bytes 35526364 | solution.py:127
  255.9 2.1 constant_dynamic-slice_fusion.3
  258.1 2.8 fusion.88
  261.0 3.3 fusion.89
  264.4 3.6 fusion.91
  268.0 2.1 constant_dynamic-slice_fusion.3
  270.2 2.8 fusion.88
  273.0 3.3 fusion.89
  276.5 3.9 fusion.91
  280.4 2.1 constant_dynamic-slice_fusion.3
  282.6 2.8 fusion.88
  285.4 3.6 fusion.89
  289.2 3.9 fusion.91
  293.1 2.1 constant_dynamic-slice_fusion.3
  295.3 2.8 fusion.88
  298.1 3.3 fusion.89
  301.6 3.9 fusion.91
  308.3 2.2 convert_element_type.105
  314.3 2.4 fusion.48
  316.7 52.9 %all-gather.13.cloned.1.call-done = bf16[256,128,128]{2,1,0:T(8,128)(2,1)} async-done(((bf16[16,128,128]{2,1,0:T(8,128)(2,1)}), bf16[256,128,128]{2,1,0:T(8,128)(2,1)}) %all-gather.13.cloned.1.call-update) | async-done | bytes 8388624 | tf_op jit(solution)/shard_map/all_gather | solution.py:21
  369.6 26.4 %while.49 = (s32[]{:T(128)}, f32[16,128,128]{2,1,0:T(8,128)S(1)}, s32[]{:T(128)}, bf16[16,16,128,128]{3,2,1,0:T(8,128)(2,1)}, s32[]{:T(128)}, /*index=5*/s32[]{:T(128)}, s32[]{:T(128)}, s32[]{:T(128)}) while((s32[]{:T(128)}, f32[16,128,128]{2,1,0:T(8,128)S(1)}, s32[]{:T(128)}, bf16[16,16,128,128]{3,2,1,0:T(8,128)(2,1)}, s32[]{:T(128)}, ...), condition=%wide.region_7.8_spmd.clone, body=%wide.region_6.7_spmd.clone.sunk | while | flops 1048584 | bytes 2621595 | solution.py:30
  396.0 2.2 convolution_bitcast_fusion.3
  398.2 3.0 fusion.18
  401.2 2.0 copy.99
  (132 shorter events, 76.5 us)
Async XLA Ops:
  7.2 1.8 copy-start
  7.2 4.8 %copy-start.10 = (bf16[128,2048]{1,0:T(8,128)(2,1)S(1)}, bf16[128,2048]{1,0:T(8,128)(2,1)}, u32[]{:S(2)}) copy-start(bf16[128,2048]{1,0:T(8,128)(2,1)} %param.15) | copy-start | bytes 1572868
  7.2 3.0 copy-start.13
  7.2 3.8 copy-start.14
  7.2 4.7 %copy-start.4 = (bf16[128,2048]{1,0:T(8,128)(2,1)S(1)}, bf16[128,2048]{1,0:T(8,128)(2,1)}, u32[]{:S(2)}) copy-start(bf16[128,2048]{1,0:T(8,128)(2,1)} %param.14) | copy-start | bytes 1572868
  7.2 119.7 %all-gather.11.cloned.1.call-start = ((), (), s32[]{:S(2)}) async-start(), calls=%async_computation.2 | async-start | bytes 8912896 | tf_op jit(solution)/shard_map/all_gather | solution.py:21
  9.0 2.9 copy-start.6
  10.2 181.6 %all-gather.7.cloned.1.call-start = ((), (), s32[]{:S(2)}) async-start(), calls=%async_computation | async-start | bytes 2228224 | tf_op jit(solution)/shard_map/all_gather | solution.py:117
  11.0 244.9 %all-gather.9.cloned.1.call-start = ((), (), s32[]{:S(2)}) async-start(), calls=%async_computation.1 | async-start | bytes 2228224 | tf_op jit(solution)/shard_map/all_gather | solution.py:118
  11.8 357.8 %all-gather.13.cloned.1.call-start = ((), (), s32[]{:S(2)}) async-start(), calls=%async_computation.3 | async-start | bytes 8912896 | tf_op jit(solution)/shard_map/all_gather | solution.py:21
  12.4 141.8 %copy-start.12 = (bf16[16,128,128]{2,1,0:T(8,128)(2,1)}, bf16[16,128,128]{2,1,0:T(8,128)(2,1)S(1)}, u32[]{:S(2)}) copy-start(bf16[16,128,128]{2,1,0:T(8,128)(2,1)S(1)} %fusion.19) | copy-start | bytes 1572868
  163.7 92.2 %copy-start.15 = (s32[128]{0:T(128)S(1)}, s32[128]{0:T(128)}, u32[]{:S(2)}) copy-start(s32[128]{0:T(128)} %param.21) | copy-start | bytes 1540
  167.3 1.3 copy-start.2
  260.9 3.5 copy-start.1
  273.0 3.5 copy-start.1
  285.4 3.8 copy-start.1
  298.1 3.5 copy-start.1
  305.5 6.7 %copy-start.3 = (bf16[128,2048]{0,1:T(8,128)(2,1)S(1)}, bf16[128,2048]{0,1:T(8,128)(2,1)}, u32[]{:S(2)}) copy-start(bf16[128,2048]{0,1:T(8,128)(2,1)} %copy-done.2) | copy-start | bytes 1572868
  310.5 2.3 copy-start.7
  312.1 1.1 copy-start.8
  369.6 28.6 %copy-start.11 = (bf16[128,2048]{1,0:T(8,128)(2,1)S(1)}, bf16[128,2048]{1,0:T(8,128)(2,1)}, u32[]{:S(2)}) copy-start(bf16[128,2048]{1,0:T(8,128)(2,1)} %param.15) | copy-start | bytes 1572868
  396.0 7.3 %copy-start.5 = (bf16[128,2048]{1,0:T(8,128)(2,1)S(1)}, bf16[128,2048]{1,0:T(8,128)(2,1)}, u32[]{:S(2)}) copy-start(bf16[128,2048]{1,0:T(8,128)(2,1)} %param.14) | copy-start | bytes 1572868
  396.0 7.3 %copy-start.9 = (bf16[16,128,128]{2,1,0:T(8,128)(2,1)S(1)}, bf16[16,128,128]{2,1,0:T(8,128)(2,1)}, u32[]{:S(2)}) copy-start(bf16[16,128,128]{2,1,0:T(8,128)(2,1)} %copy-done.8) | copy-start | bytes 1572868
Sparse Core Ops, SparseCore 0:
  11.4 115.5 all-gather.10
  130.2 61.4 all-gather.6
  194.4 61.4 all-gather.8
  258.5 111.0 all-gather.12
where the time goes:
time: 415 us; the launch traced here: 412 us
  waiting for transfers between devices  251 us (60%)
  other arithmetic  71.4 us (17%)
  matrix products  42.6 us (10%)
  local copies, waits for them, and re-layouts  26.8 us (6%)
  between operations  14.1 us (3%)
  blocking collectives  5.11 us (1%)
    all_gather x2, waiting for transfers between devices, carried_in(): everything = lax.all_gather(value.astype(jnp.bfloat16), axis)  167 us
    all_gather x1, waiting for transfers between devices, on_device(): value_rows = lax.all_gather(soft_value, 'ctx', axis=0, tiled=True)  64.2 us
    select_n x32, other arithmetic, hop(): return jnp.where(reached, new, before)  51.8 us
    all_gather x1, waiting for transfers between devices, on_device(): key_rows = lax.all_gather(soft_key, 'ctx', axis=0, tiled=True)  19.6 us
    dot_general x4, matrix products, attend(): jnp.einsum('kgtn,nkd->kgtd', probs.astype(jnp.bfloat16), value_heads, pre...  15.2 us
    reduce_sum x4, other arithmetic, attend(): new_total = shrink * old_total + jnp.sum(probs, axis=-1)  13.6 us
    dot_general x4, matrix products, attend(): jnp.einsum('tkgd,nkd->kgtn', soft_q, key_heads, preferred_element_type=jn...  11.2 us
    unnamed x38, local copies, waits for them, and re-layouts  10.3 us
  transfers between devices with their start and end apart: 4, of which 4 were waited for; matrix products, arithmetic and copies ran while one was open for 25% of the time, Pallas kernels for 0%

commit v1 on v0

v1 whole, which is shorter than its diff:
```python
import functools
import math

import jax
import jax.numpy as jnp
from jax import lax
from jax.experimental import pallas as pl
from jax.experimental.pallas import tpu as pltpu
from jax.sharding import PartitionSpec as P

HD = 128
G = 4

MESH = pl.DeviceIdType.MESH
epsilon = 1e-06
floor_score = -1e30
f32 = jnp.float32
bf16 = jnp.bfloat16


def dot(a, b, ca, cb):
    return lax.dot_general(a, b, (((ca,), (cb,)), ((), ())), preferred_element_type=f32)


def kernel(
    n,
    n_tp,
    lq, lk, lv, lg, sq, sk, sv, doc,
    lin_out, grad_q, grad_k, grad_v, soft_out,
    st_own, st_in, st_tot, st_z, st_out, st_fin,
    scores, mix, gmix, gk_acc, gv_acc,
    ex_own, ex_in,
    kv, q_in, q_rows, doc_in, o_own, top, total, acc,
    a_send, a_recv, z_send, z_recv, c_send, c_recv,
    e_send, e_recv, s_send, s_recv, kvz_send, kvz_recv, o_send, o_recv,
):
    length = lq.shape[0]
    heads = lq.shape[1] // HD
    hq = heads // G
    planes = n // G
    q_heads = sq.shape[1] // HD
    kv_heads = sk.shape[1] // HD
    mine = q_heads // G
    qw = mine * HD
    unit = min(4, heads)
    me = lax.axis_index("ctx")
    tp = lax.axis_index("tp")
    z = me // G
    p = lax.rem(me, G)

    def member(d):
        return lax.rem(p + d, G)

    def at_member(r):
        return {"ctx": z * G + r}

    def at_plane(zz):
        return {"ctx": zz * G + p}

    def remote(src, dst, send, recv, device):
        return pltpu.make_async_remote_copy(
            src_ref=src, dst_ref=dst, send_sem=send, recv_sem=recv,
            device_id=device, device_id_type=MESH,
        )

    barrier = pltpu.get_barrier_semaphore()
    for d in range(1, G):
        pl.semaphore_signal(barrier, inc=1, device_id=at_member(member(d)), device_id_type=MESH)
    for k in range(1, planes):
        pl.semaphore_signal(
            barrier, inc=1, device_id=at_plane(lax.rem(z + k, planes)), device_id_type=MESH
        )
    for k in range(1, n_tp):
        pl.semaphore_signal(
            barrier, inc=1, device_id={"tp": lax.rem(tp + k, n_tp)}, device_id_type=MESH
        )

    def lanes(h):
        return pl.ds(pl.multiple_of(h * HD, HD), HD)

    def per_heads(body):
        def step(i, _):
            body([i * unit + u for u in range(unit)])
            return 0

        lax.fori_loop(0, heads // unit, step, 0)

    def outer_states(way, left, right):
        def body(hs):
            ls = [left[:, lanes(h)] for h in hs]
            rs = [right[:, lanes(h)] for h in hs]
            out = [dot(a, b, 0, 0).astype(bf16) for a, b in zip(ls, rs)]
            for h, o in zip(hs, out):
                st_own[way, h] = o

        per_heads(body)

    outer_states(0, lk, lv)
    pl.semaphore_wait(barrier, (G - 1) + (planes - 1) + (n_tp - 1))

    def scan_a(way):
        return [
            remote(
                st_own.at[way, pl.ds(member(d) * hq, hq)], st_in.at[way, p],
                a_send.at[way, d - 1], a_recv.at[way, d - 1], at_member(member(d)),
            )
            for d in range(1, G)
        ]

    def scan_z(way, k):
        there = z - k if way else z + k
        return remote(
            st_tot.at[way], st_z.at[way, k - 1],
            z_send.at[way, k - 1], z_recv.at[way, k - 1], at_plane(there),
        )

    def sends_z(way, k):
        return (z - k >= 0) if way else (z + k < planes)

    def scan_c(way):
        return [
            remote(
                st_out.at[way, member(d)], st_fin.at[way, pl.ds(p * hq, hq)],
                c_send.at[way, d - 1], c_recv.at[way, d - 1], at_member(member(d)),
            )
            for d in range(1, G)
        ]

    def scan_start(way):
        for copy in scan_a(way):
            copy.start()
        st_in[way, p] = st_own[way, pl.ds(p * hq, hq)]

    def scan_middle(way):
        for copy in scan_a(way):
            copy.wait_recv()
        for h in range(hq):
            parts = [st_in[way, s, h].astype(f32) for s in range(G)]
            st_tot[way, h] = ((parts[0] + parts[1]) + (parts[2] + parts[3])).astype(bf16)
        for k in range(1, planes):

            @pl.when(sends_z(way, k))
            def _():
                scan_z(way, k).start()

    def scan_end(way):
        for k in range(1, planes):

            @pl.when(sends_z(1 - way, k))
            def _():
                scan_z(way, k).wait_recv()

        for h in range(hq):
            carry = jnp.zeros((HD, HD), f32)
            for k in range(1, planes):
                here = jnp.where(sends_z(1 - way, k), 1.0, 0.0)
                got = st_z[way, k - 1, h].astype(f32)
                carry = carry + jnp.where(here > 0.5, got, 0.0)
            order = range(G - 1, -1, -1) if way else range(G)
            for s in order:
                st_out[way, s, h] = carry.astype(bf16)
                carry = carry + st_in[way, s, h].astype(f32)
        for copy in scan_c(way):
            copy.start()
        st_fin[way, pl.ds(p * hq, hq)] = st_out[way, p]

    def scan_done(way):
        for copy in scan_c(way):
            copy.wait_recv()

    scan_start(0)

    def kv_lanes(r):
        return pl.ds(pl.multiple_of((r * kv_heads // G) * HD, HD), HD)

    def soft_copies():
        out = []
        for d in range(1, G):
            r = member(d)
            rows = pl.ds(p * length, length)
            for i, (src, dst) in enumerate(
                (
                    (sk.at[:, kv_lanes(r)], kv.at[z, 0, rows]),
                    (sv.at[:, kv_lanes(r)], kv.at[z, 1, rows]),
                    (doc, doc_in.at[p]),
                    (sq.at[:, pl.ds(pl.multiple_of(r * qw, HD), qw)], q_in.at[p]),
                )
            ):
                out.append(
                    remote(src, dst, s_send.at[d - 1, i], s_recv.at[d - 1, i], at_member(r))
                )
        return out

    for copy in soft_copies():
        copy.start()
    own_rows = pl.ds(pl.multiple_of(p * length, length), length)
    kv[z, 0, own_rows] = sk[:, kv_lanes(p)]
    kv[z, 1, own_rows] = sv[:, kv_lanes(p)]
    doc_in[p] = doc[...]
    q_in[p] = sq[:, pl.ds(pl.multiple_of(p * qw, HD), qw)]

    lower = lax.broadcasted_iota(jnp.int32, (length, length), 0) >= lax.broadcasted_iota(
        jnp.int32, (length, length), 1
    )

    def intra_forward(hs):
        qs = [lq[:, lanes(h)] for h in hs]
        ks = [lk[:, lanes(h)] for h in hs]
        vs = [lv[:, lanes(h)] for h in hs]
        ws = [jnp.where(lower, dot(a, b, 1, 1), 0.0).astype(bf16) for a, b in zip(qs, ks)]
        ms = [dot(w, v, 1, 0) for w, v in zip(ws, vs)]
        for h, w, m in zip(hs, ws, ms):
            scores[h] = w
            mix[:, lanes(h)] = m

    per_heads(intra_forward)
    scan_middle(0)

    for copy in soft_copies():
        copy.wait_recv()

    def kv_copy(k):
        return remote(
            kv.at[z], kv.at[z], kvz_send.at[k - 1], kvz_recv.at[k - 1], at_plane(z + k)
        )

    def kv_arrival(k):
        return remote(
            kv.at[z - k], kv.at[z - k], kvz_send.at[k - 1], kvz_recv.at[k - 1], at_plane(z - k)
        )

    for k in range(1, planes):

        @pl.when(z + k < planes)
        def _():
            kv_copy(k).start()

    span = G * length
    factor = math.log2(math.e) / math.sqrt(HD)

    def tile(b, zz, first):
        keys = kv[zz, 0]
        vals = kv[zz, 1]
        raw = dot(keys, q_rows[b], 1, 1) * factor
        key_pos = zz * span + lax.broadcasted_iota(jnp.int32, (span, qw), 0)
        begins = jnp.concatenate([doc_in[b][0:1, :]] * mine, axis=1)
        allowed = key_pos >= begins
        if first:
            one = lax.broadcasted_iota(jnp.int32, (1, length), 1)
            q_pos = z * span + b * length + jnp.concatenate([one] * mine, axis=1)
            allowed = allowed & (key_pos <= q_pos)
        raw = jnp.where(allowed, raw, floor_score)
        high = jnp.max(raw, axis=0, keepdims=True)
        if not first:
            old = top[b]
            high = jnp.maximum(old, high)
            shrink = jnp.exp2(old - high)
        probs = jnp.exp2(raw - high)
        summed = jnp.sum(probs, axis=0, keepdims=True)
        update = dot(vals, probs.astype(bf16), 0, 0)
        top[b] = high
        if first:
            total[b] = summed
            acc[b] = update
        else:
            total[b] = total[b] * shrink + summed
            acc[b] = acc[b] * shrink + update

    def own_tile(b, _):
        for h in range(mine):
            q_rows[b, h * length : (h + 1) * length, :] = q_in[b, :, h * HD : (h + 1) * HD]
        tile(b, z, True)
        return 0

    lax.fori_loop(0, G, own_tile, 0)
    scan_end(0)
    scan_done(0)

    ex_own[...] = jnp.zeros_like(ex_own)

    def inter_forward(hs):
        qs = [lq[:, lanes(h)] for h in hs]
        ss = [st_fin[0, h] for h in hs]
        ms = [mix[:, lanes(h)] + dot(a, s, 1, 0) for h, a, s in zip(hs, qs, ss)]
        gs = [lg[:, lanes(h)].astype(f32) for h in hs]
        square, inner = ex_own[0], ex_own[1]
        for m, g in zip(ms, gs):
            square = square + m * m
            inner = inner + g * m
        ex_own[0] = square
        ex_own[1] = inner
        for h, m in zip(hs, ms):
            mix[:, lanes(h)] = m

    per_heads(inter_forward)

    def exchange():
        return [
            remote(
                ex_own, ex_in.at[k - 1], e_send.at[k - 1], e_recv.at[k - 1],
                {"tp": lax.rem(tp + k, n_tp)},
            )
            for k in range(1, n_tp)
        ]

    for copy in exchange():
        copy.start()
    for copy in exchange():
        copy.wait_recv()
    square, inner = ex_own[0], ex_own[1]
    for k in range(n_tp - 1):
        square = square + ex_in[k, 0]
        inner = inner + ex_in[k, 1]
    features = heads * HD * n_tp
    scale = lax.rsqrt(jnp.sum(square, axis=1, keepdims=True) / features + epsilon)
    mean = scale * jnp.sum(inner, axis=1, keepdims=True) / features

    def turn(hs):
        qs = [lq[:, lanes(h)] for h in hs]
        ns = [mix[:, lanes(h)] * scale for h in hs]
        gs = [(scale * (lg[:, lanes(h)].astype(f32) - m * mean)).astype(bf16) for h, m in zip(hs, ns)]
        adj = [dot(a, g, 0, 0).astype(bf16) for a, g in zip(qs, gs)]
        for h, m, g, o in zip(hs, ns, gs, adj):
            lin_out[:, lanes(h)] = m.astype(bf16)
            gmix[:, lanes(h)] = g
            st_own[1, h] = o

    per_heads(turn)
    scan_start(1)

    def intra_backward(hs):
        qs = [lq[:, lanes(h)] for h in hs]
        ks = [lk[:, lanes(h)] for h in hs]
        vs = [lv[:, lanes(h)] for h in hs]
        gs = [gmix[:, lanes(h)] for h in hs]
        ss = [st_fin[0, h] for h in hs]
        ws = [scores[h] for h in hs]
        ds = [jnp.where(lower, dot(g, v, 1, 1), 0.0).astype(bf16) for g, v in zip(gs, vs)]
        gq = [dot(d, k, 1, 0) + dot(g, s, 1, 1) for d, k, g, s in zip(ds, ks, gs, ss)]
        gk = [dot(d, q, 0, 0) for d, q in zip(ds, qs)]
        gv = [dot(w, g, 0, 0) for w, g in zip(ws, gs)]
        for h, a, b, c in zip(hs, gq, gk, gv):
            grad_q[:, lanes(h)] = a.astype(bf16)
            gk_acc[:, lanes(h)] = b
            gv_acc[:, lanes(h)] = c

    per_heads(intra_backward)
    scan_middle(1)

    def earlier_plane(k, _):
        kv_arrival(k).wait_recv()

        def one(b, _):
            tile(b, z - k, False)
            return 0

        lax.fori_loop(0, G, one, 0)
        return 0

    lax.fori_loop(1, z + 1, earlier_plane, 0)
    scan_end(1)

    def finish(b, _):
        out = acc[b] / total[b]
        for h in range(mine):
            o_own[b, :, h * HD : (h + 1) * HD] = jnp.transpose(
                out[:, h * length : (h + 1) * length]
            ).astype(bf16)
        return 0

    lax.fori_loop(0, G, finish, 0)

    def out_copies():
        return [
            remote(
                o_own.at[member(d)], soft_out.at[:, pl.ds(pl.multiple_of(p * qw, HD), qw)],
                o_send.at[d - 1], o_recv.at[d - 1], at_member(member(d)),
            )
            for d in range(1, G)
        ]

    for copy in out_copies():
        copy.start()
    soft_out[:, pl.ds(pl.multiple_of(p * qw, HD), qw)] = o_own[p]
    scan_done(1)

    def inter_backward(hs):
        ks = [lk[:, lanes(h)] for h in hs]
        vs = [lv[:, lanes(h)] for h in hs]
        ss = [st_fin[1, h] for h in hs]
        gk = [gk_acc[:, lanes(h)] + dot(v, s, 1, 1) for h, v, s in zip(hs, vs, ss)]
        gv = [gv_acc[:, lanes(h)] + dot(k, s, 1, 0) for h, k, s in zip(hs, ks, ss)]
        for h, a, b in zip(hs, gk, gv):
            grad_k[:, lanes(h)] = a.astype(bf16)
            grad_v[:, lanes(h)] = b.astype(bf16)

    per_heads(inter_backward)

    for copy in out_copies():
        copy.wait_recv()
    for copy in scan_a(0) + scan_a(1) + scan_c(0) + scan_c(1):
        copy.wait_send()
    for copy in soft_copies() + exchange() + out_copies():
        copy.wait_send()
    for k in range(1, planes):

        @pl.when(z + k < planes)
        def _():
            kv_copy(k).wait_send()

        for way in (0, 1):

            @pl.when(sends_z(way, k))
            def _():
                scan_z(way, k).wait_send()


def on_device(n, n_tp, lq, lk, lv, lg, sq, sk, sv, doc_start):
    length, width = lq.shape
    heads = width // HD
    hq = heads // G
    planes = n // G
    q_width = sq.shape[1]
    qw = q_width // G
    doc = jnp.broadcast_to(doc_start[None, :], (8, length))
    dma = pltpu.SemaphoreType.DMA
    vm = pltpu.VMEM
    span = G * length
    others = planes - 1
    scratch = [
        vm((2, heads, HD, HD), bf16),
        vm((2, G, hq, HD, HD), bf16),
        vm((2, hq, HD, HD), bf16),
        vm((2, others, hq, HD, HD), bf16),
        vm((2, G, hq, HD, HD), bf16),
        vm((2, heads, HD, HD), bf16),
        vm((heads, length, length), bf16),
        vm((length, width), f32),
        vm((length, width), bf16),
        vm((length, width), f32),
        vm((length, width), f32),
        vm((2, length, HD), f32),
        vm((n_tp - 1, 2, length, HD), f32),
        vm((planes, 2, span, HD), bf16),
        vm((G, length, qw), bf16),
        vm((G, qw // HD * length, HD), bf16),
        vm((G, 8, length), jnp.int32),
        vm((G, length, qw), bf16),
        vm((G, 1, qw), f32),
        vm((G, 1, qw), f32),
        vm((G, HD, qw), f32),
        dma((2, G - 1)), dma((2, G - 1)),
        dma((2, others)), dma((2, others)),
        dma((2, G - 1)), dma((2, G - 1)),
        dma((n_tp - 1,)), dma((n_tp - 1,)),
        dma((G - 1, 4)), dma((G - 1, 4)),
        dma((others,)), dma((others,)),
        dma((G - 1,)), dma((G - 1,)),
    ]
    shape = jax.ShapeDtypeStruct((length, width), bf16)
    return pl.pallas_call(
        functools.partial(kernel, n, n_tp),
        out_shape=[shape] * 4 + [jax.ShapeDtypeStruct((length, q_width), bf16)],
        in_specs=[pl.BlockSpec(memory_space=pltpu.VMEM)] * 8,
        out_specs=[pl.BlockSpec(memory_space=pltpu.VMEM)] * 5,
        scratch_shapes=scratch,
        compiler_params=pltpu.CompilerParams(
            collective_id=0, has_side_effects=True, vmem_limit_bytes=48 * 1024 * 1024
        ),
    )(lq, lk, lv, lg, sq, sk, sv, doc)


def solution(mesh):
    wide = P("ctx", "tp")
    return jax.shard_map(
        functools.partial(on_device, mesh.shape["ctx"], mesh.shape["tp"]),
        mesh=mesh,
        in_specs=(wide,) * 7 + (P("ctx"),),
        out_specs=(wide,) * 5,
        check_vma=False,
    )
```

time: 415 us -> 81.2 us (0.20)
  waiting for transfers between devices: 251 us -> 0 us
  other arithmetic: 71.4 us -> 0 us
  Pallas kernels: 0 us -> 68.6 us
  matrix products: 42.6 us -> 0 us
  local copies, waits for them, and re-layouts: 26.8 us -> 11.6 us
  between operations: 14.1 us -> 0.65 us
  blocking collectives: 5.11 us -> 0 us
    all_gather x4 -> x0, waiting for transfers between devices: 251 us -> none  [the longest x2 167 us: carried_in(): everything = lax.all_gather(value.astype(jnp.bfloat16), axis)]
    pallas_call x0 -> x1, Pallas kernels: none -> 68.6 us  [on_device(): pl.pallas_call(functools.partial(kernel, n, n_tp), out_shape=[shape] * 4...]
    select_n x32 -> x0, other arithmetic: 51.8 us -> none  [hop(): return jnp.where(reached, new, before)]
    dot_general x20 -> x0, matrix products: 42.6 us -> none  [the longest x4 15.2 us: attend(): jnp.einsum('kgtn,nkd->kgtd', probs.astype(jnp.bfloat16), value_heads, pre...]
    reduce_sum x5 -> x0, other arithmetic: 15 us -> none  [the longest x4 13.6 us: attend(): new_total = shrink * old_total + jnp.sum(probs, axis=-1)]
    dynamic_slice x4 -> x0, local copies, waits for them, and re-layouts: 8.26 us -> none  [inner_step(): value_part = lax.dynamic_slice_in_dim(value_rows, index * block, block, 0)]
    psum x2 -> x0, blocking collectives: 5.11 us -> none  [the longest x1 2.64 us: on_device(): inner = lax.psum(jnp.sum(grad * normed, axis=1), 'tp')]
    convert_element_type x3 -> x0, local copies, waits for them, and re-layouts: 4.43 us -> none  [the longest x2 3.42 us: on_device(): soft_out = jnp.transpose(result, (2, 0, 1, 3)).reshape(length, kv_here *...]
  transfers between devices with their start and end apart: 4 -> 0, of which waited for: 4 -> 0; matrix products, arithmetic and copies ran while one was open for 25% -> 0% of each run, Pallas kernels for 0% -> 0%
where the time goes in v1:
time: 81.2 us; the launch traced here: 80.8 us
  Pallas kernels  68.6 us (84%)
  local copies, waits for them, and re-layouts  11.6 us (14%)
    pallas_call x1, Pallas kernels, on_device(): pl.pallas_call(functools.partial(kernel, n, n_tp), out_shape=[shape] * 4...  68.6 us
    unnamed x19, local copies, waits for them, and re-layouts  11 us

profile of v1, /device:TPU:0, one launch (start us, length us, event | category | flops | bytes accessed | tf_op | source)
XLA Modules:
  0.0 80.8 jit_solution(3322378820871449004)
XLA Ops:
  0.6 0.7 broadcast_in_dim.2.doc
  1.3 0.0 copy-start
  1.3 1.0 %copy-done = bf16[128,2048]{1,0:T(8,128)(2,1)S(1)} copy-done((bf16[128,2048]{1,0:T(8,128)(2,1)S(1)}, bf16[128,2048]{1,0:T(8,128)(2,1)}, u32[]{:S(2)}) %copy-start) | copy-done | bytes 524312
  2.3 0.0 copy-start.1
  2.3 1.0 %copy-done.1 = bf16[128,2048]{1,0:T(8,128)(2,1)S(1)} copy-done((bf16[128,2048]{1,0:T(8,128)(2,1)S(1)}, bf16[128,2048]{1,0:T(8,128)(2,1)}, u32[]{:S(2)}) %copy-start.1) | copy-done | bytes 524312
  3.4 0.0 copy-start.2
  3.4 1.0 %copy-done.2 = bf16[128,2048]{1,0:T(8,128)(2,1)S(1)} copy-done((bf16[128,2048]{1,0:T(8,128)(2,1)S(1)}, bf16[128,2048]{1,0:T(8,128)(2,1)}, u32[]{:S(2)}) %copy-start.2) | copy-done | bytes 524312
  4.4 0.0 copy-start.3
  4.4 1.0 %copy-done.3 = bf16[128,2048]{1,0:T(8,128)(2,1)S(1)} copy-done((bf16[128,2048]{1,0:T(8,128)(2,1)S(1)}, bf16[128,2048]{1,0:T(8,128)(2,1)}, u32[]{:S(2)}) %copy-start.3) | copy-done | bytes 524312
  5.5 0.0 copy-start.4
  5.5 1.0 %copy-done.4 = bf16[128,2048]{1,0:T(8,128)(2,1)S(1)} copy-done((bf16[128,2048]{1,0:T(8,128)(2,1)S(1)}, bf16[128,2048]{1,0:T(8,128)(2,1)}, u32[]{:S(2)}) %copy-start.4) | copy-done | bytes 524312
  6.5 0.0 copy-start.5
  6.5 0.9 %copy-done.5 = bf16[128,512]{1,0:T(8,128)(2,1)S(1)} copy-done((bf16[128,512]{1,0:T(8,128)(2,1)S(1)}, bf16[128,512]{1,0:T(8,128)(2,1)}, u32[]{:S(2)}) %copy-start.5) | copy-done | bytes 131096
  7.4 0.0 copy-start.6
  7.4 0.9 %copy-done.6 = bf16[128,512]{1,0:T(8,128)(2,1)S(1)} copy-done((bf16[128,512]{1,0:T(8,128)(2,1)S(1)}, bf16[128,512]{1,0:T(8,128)(2,1)}, u32[]{:S(2)}) %copy-start.6) | copy-done | bytes 131096
  8.3 68.6 %shard_map.119 = (bf16[128,2048]{1,0:T(8,128)(2,1)S(1)}, bf16[128,2048]{1,0:T(8,128)(2,1)S(1)}, bf16[128,2048]{1,0:T(8,128)(2,1)S(1)}, bf16[128,2048]{1,0:T(8,128)(2,1)S(1)}, bf16[128,2048]{1,0:T(8,128)(2,1)S(1)}) custom-call(bf16[128,2048]{1,0:T(8,128)(2,1)S(1)} %copy-done, bf16[128,2048]{1,0:T(8,128)(2,1)S(1)} %copy-done.1, ...), custom_call_target="tpu_custom_call" | custom-call | tf_op jit(solution)/shard_map/pallas_call | solution.py:461
  76.9 0.8 copy.18
  77.7 0.8 copy.19
  78.5 0.8 copy.20
  79.3 0.8 copy.21
  80.1 0.8 copy.22
Async XLA Ops:
  1.3 1.0 %copy-start = (bf16[128,2048]{1,0:T(8,128)(2,1)S(1)}, bf16[128,2048]{1,0:T(8,128)(2,1)}, u32[]{:S(2)}) copy-start(bf16[128,2048]{1,0:T(8,128)(2,1)} %lq.1) | copy-start | bytes 1572868
  2.3 1.0 %copy-start.1 = (bf16[128,2048]{1,0:T(8,128)(2,1)S(1)}, bf16[128,2048]{1,0:T(8,128)(2,1)}, u32[]{:S(2)}) copy-start(bf16[128,2048]{1,0:T(8,128)(2,1)} %lk.1) | copy-start | bytes 1572868
  3.4 1.0 %copy-start.2 = (bf16[128,2048]{1,0:T(8,128)(2,1)S(1)}, bf16[128,2048]{1,0:T(8,128)(2,1)}, u32[]{:S(2)}) copy-start(bf16[128,2048]{1,0:T(8,128)(2,1)} %lv.1) | copy-start | bytes 1572868
  4.4 1.0 %copy-start.3 = (bf16[128,2048]{1,0:T(8,128)(2,1)S(1)}, bf16[128,2048]{1,0:T(8,128)(2,1)}, u32[]{:S(2)}) copy-start(bf16[128,2048]{1,0:T(8,128)(2,1)} %lg.1) | copy-start | bytes 1572868
  5.5 1.0 %copy-start.4 = (bf16[128,2048]{1,0:T(8,128)(2,1)S(1)}, bf16[128,2048]{1,0:T(8,128)(2,1)}, u32[]{:S(2)}) copy-start(bf16[128,2048]{1,0:T(8,128)(2,1)} %sq.1) | copy-start | bytes 1572868
  6.5 0.9 %copy-start.5 = (bf16[128,512]{1,0:T(8,128)(2,1)S(1)}, bf16[128,512]{1,0:T(8,128)(2,1)}, u32[]{:S(2)}) copy-start(bf16[128,512]{1,0:T(8,128)(2,1)} %sk.1) | copy-start | bytes 393220
  7.4 0.9 %copy-start.6 = (bf16[128,512]{1,0:T(8,128)(2,1)S(1)}, bf16[128,512]{1,0:T(8,128)(2,1)}, u32[]{:S(2)}) copy-start(bf16[128,512]{1,0:T(8,128)(2,1)} %sv.1) | copy-start | bytes 393220

commit v2 on v1

--- a/solution.py
+++ b/solution.py
@@ -25,15 +25,27 @@
 def kernel(
     n,
     n_tp,
-    lq, lk, lv, lg, sq, sk, sv, doc,
+    lq_hbm, lk_hbm, lv_hbm, lg_hbm, sq_hbm, sk_hbm, sv_hbm, doc_row,
     lin_out, grad_q, grad_k, grad_v, soft_out,
+    lq, lk, lv, lg, sq, sk, sv, doc, in_sems,
     st_own, st_in, st_tot, st_z, st_out, st_fin,
     scores, mix, gmix, gk_acc, gv_acc,
     ex_own, ex_in,
-    kv, q_in, q_rows, doc_in, o_own, top, total, acc,
+    kv, q_in, q_rows, doc_in, o_own, top, total, acc, carry_ref,
     a_send, a_recv, z_send, z_recv, c_send, c_recv,
     e_send, e_recv, s_send, s_recv, kvz_send, kvz_recv, o_send, o_recv,
 ):
+    loads = [
+        pltpu.make_async_copy(src, dst, in_sems.at[i])
+        for i, (src, dst) in enumerate(
+            (
+                (lk_hbm, lk), (lv_hbm, lv), (lq_hbm, lq), (sk_hbm, sk),
+                (sv_hbm, sv), (sq_hbm, sq), (lg_hbm, lg),
+            )
+        )
+    ]
+    for copy in loads:
+        copy.start()
     length = lq.shape[0]
     heads = lq.shape[1] // HD
     hq = heads // G
@@ -42,7 +54,6 @@
     kv_heads = sk.shape[1] // HD
     mine = q_heads // G
     qw = mine * HD
-    unit = min(4, heads)
     me = lax.axis_index("ctx")
     tp = lax.axis_index("tp")
     z = me // G
@@ -78,121 +89,121 @@
     def lanes(h):
         return pl.ds(pl.multiple_of(h * HD, HD), HD)
 
-    def per_heads(body):
-        def step(i, _):
-            body([i * unit + u for u in range(unit)])
+    def chunk_heads(c):
+        return [r * hq + c for r in range(G)]
+
+    def per_chunk(body):
+        for c in range(hq):
+            body(chunk_heads(c))
+
+    def per_chunk_loop(body):
+        def step(c, _):
+            body(chunk_heads(c))
             return 0
 
-        lax.fori_loop(0, heads // unit, step, 0)
-
-    def outer_states(way, left, right):
-        def body(hs):
-            ls = [left[:, lanes(h)] for h in hs]
-            rs = [right[:, lanes(h)] for h in hs]
-            out = [dot(a, b, 0, 0).astype(bf16) for a, b in zip(ls, rs)]
-            for h, o in zip(hs, out):
-                st_own[way, h] = o
-
-        per_heads(body)
-
-    outer_states(0, lk, lv)
-    pl.semaphore_wait(barrier, (G - 1) + (planes - 1) + (n_tp - 1))
-
-    def scan_a(way):
+        lax.fori_loop(0, hq, step, 0)
+
+    def scan_a(way, c):
         return [
             remote(
-                st_own.at[way, pl.ds(member(d) * hq, hq)], st_in.at[way, p],
-                a_send.at[way, d - 1], a_recv.at[way, d - 1], at_member(member(d)),
+                st_own.at[way, member(d) * hq + c], st_in.at[way, p, c],
+                a_send.at[way, d - 1, c], a_recv.at[way, d - 1, c], at_member(member(d)),
             )
             for d in range(1, G)
         ]
 
-    def scan_z(way, k):
+    def scan_z(way, k, c):
         there = z - k if way else z + k
         return remote(
-            st_tot.at[way], st_z.at[way, k - 1],
-            z_send.at[way, k - 1], z_recv.at[way, k - 1], at_plane(there),
+            st_tot.at[way, c], st_z.at[way, k - 1, c],
+            z_send.at[way, k - 1, c], z_recv.at[way, k - 1, c], at_plane(there),
         )
 
     def sends_z(way, k):
         return (z - k >= 0) if way else (z + k < planes)
 
-    def scan_c(way):
+    def scan_c(way, c):
         return [
             remote(
-                st_out.at[way, member(d)], st_fin.at[way, pl.ds(p * hq, hq)],
-                c_send.at[way, d - 1], c_recv.at[way, d - 1], at_member(member(d)),
+                st_out.at[way, member(d), c], st_fin.at[way, p * hq + c],
+                c_send.at[way, d - 1, c], c_recv.at[way, d - 1, c], at_member(member(d)),
             )
             for d in range(1, G)
         ]
 
-    def scan_start(way):
-        for copy in scan_a(way):
+    def scan_start(way, c):
+        for copy in scan_a(way, c):
             copy.start()
-        st_in[way, p] = st_own[way, pl.ds(p * hq, hq)]
-
-    def scan_middle(way):
-        for copy in scan_a(way):
+        st_in[way, p, c] = st_own[way, p * hq + c]
+
+    def scan_middle(way, c):
+        for copy in scan_a(way, c):
             copy.wait_recv()
-        for h in range(hq):
-            parts = [st_in[way, s, h].astype(f32) for s in range(G)]
-            st_tot[way, h] = ((parts[0] + parts[1]) + (parts[2] + parts[3])).astype(bf16)
+        parts = [st_in[way, s, c].astype(f32) for s in range(G)]
+        st_tot[way, c] = ((parts[0] + parts[1]) + (parts[2] + parts[3])).astype(bf16)
         for k in range(1, planes):
 
             @pl.when(sends_z(way, k))
             def _():
-                scan_z(way, k).start()
-
-    def scan_end(way):
+                scan_z(way, k, c).start()
+
+    def scan_end(way, c):
+        carry_ref[...] = jnp.zeros((HD, HD), f32)
         for k in range(1, planes):
 
             @pl.when(sends_z(1 - way, k))
             def _():
-                scan_z(way, k).wait_recv()
-
-        for h in range(hq):
-            carry = jnp.zeros((HD, HD), f32)
-            for k in range(1, planes):
-                here = jnp.where(sends_z(1 - way, k), 1.0, 0.0)
-                got = st_z[way, k - 1, h].astype(f32)
-                carry = carry + jnp.where(here > 0.5, got, 0.0)
-            order = range(G - 1, -1, -1) if way else range(G)
-            for s in order:
-                st_out[way, s, h] = carry.astype(bf16)
-                carry = carry + st_in[way, s, h].astype(f32)
-        for copy in scan_c(way):
+                scan_z(way, k, c).wait_recv()
+                carry_ref[...] += st_z[way, k - 1, c].astype(f32)
+
+        carry = carry_ref[...]
+        order = range(G - 1, -1, -1) if way else range(G)
+        for s in order:
+            st_out[way, s, c] = carry.astype(bf16)
+            carry = carry + st_in[way, s, c].astype(f32)
+        for copy in scan_c(way, c):
             copy.start()
-        st_fin[way, pl.ds(p * hq, hq)] = st_out[way, p]
-
-    def scan_done(way):
-        for copy in scan_c(way):
+        st_fin[way, p * hq + c] = st_out[way, p, c]
+
+    def scan_done(way, c):
+        for copy in scan_c(way, c):
             copy.wait_recv()
 
-    scan_start(0)
+    loads[0].wait()
+    loads[1].wait()
+    doc[...] = jnp.broadcast_to(doc_row[...], doc.shape)
+    for c in range(hq):
+        hs = chunk_heads(c)
+        outs = [dot(lk[:, lanes(h)], lv[:, lanes(h)], 0, 0).astype(bf16) for h in hs]
+        for h, o in zip(hs, outs):
+            st_own[0, h] = o
+        if c == 0:
+            pl.semaphore_wait(barrier, (G - 1) + (planes - 1) + (n_tp - 1))
+        scan_start(0, c)
 
     def kv_lanes(r):
         return pl.ds(pl.multiple_of((r * kv_heads // G) * HD, HD), HD)
 
-    def soft_copies():
+    def soft_copies(which):
         out = []
         for d in range(1, G):
             r = member(d)
-            rows = pl.ds(p * length, length)
-            for i, (src, dst) in enumerate(
-                (
-                    (sk.at[:, kv_lanes(r)], kv.at[z, 0, rows]),
-                    (sv.at[:, kv_lanes(r)], kv.at[z, 1, rows]),
-                    (doc, doc_in.at[p]),
-                    (sq.at[:, pl.ds(pl.multiple_of(r * qw, HD), qw)], q_in.at[p]),
-                )
-            ):
+            rows = pl.ds(pl.multiple_of(p * length, length), length)
+            refs = (
+                (sk.at[:, kv_lanes(r)], kv.at[z, 0, rows]),
+                (sv.at[:, kv_lanes(r)], kv.at[z, 1, rows]),
+                (doc, doc_in.at[p]),
+                (sq.at[:, pl.ds(pl.multiple_of(r * qw, HD), qw)], q_in.at[p]),
+            )
+            for i in which:
+                src, dst = refs[i]
                 out.append(
                     remote(src, dst, s_send.at[d - 1, i], s_recv.at[d - 1, i], at_member(r))
                 )
         return out
 
-    for copy in soft_copies():
-        copy.start()
+    for load in loads[2:6]:
+        load.wait()
     own_rows = pl.ds(pl.multiple_of(p * length, length), length)
     kv[z, 0, own_rows] = sk[:, kv_lanes(p)]
     kv[z, 1, own_rows] = sv[:, kv_lanes(p)]
@@ -213,10 +224,15 @@
             scores[h] = w
             mix[:, lanes(h)] = m
 
-    per_heads(intra_forward)
-    scan_middle(0)
-
-    for copy in soft_copies():
+    for c in range(hq):
+        intra_forward(chunk_heads(c))
+        scan_middle(0, c)
+        if c == (hq - 1) // 2:
+            for copy in soft_copies((0, 1, 2)):
+                copy.start()
+    for copy in soft_copies((3,)):
+        copy.start()
+    for copy in soft_copies((0, 1, 2)):
         copy.wait_recv()
 
     def kv_copy(k):
@@ -272,9 +288,9 @@
         tile(b, z, True)
         return 0
 
-    lax.fori_loop(0, G, own_tile, 0)
-    scan_end(0)
-    scan_done(0)
+    for c in range(hq):
+        scan_end(0, c)
+    loads[6].wait()
 
     ex_own[...] = jnp.zeros_like(ex_own)
 
@@ -292,7 +308,9 @@
         for h, m in zip(hs, ms):
             mix[:, lanes(h)] = m
 
-    per_heads(inter_forward)
+    for c in range(hq):
+        scan_done(0, c)
+        inter_forward(chunk_heads(c))
 
     def exchange():
         return [
@@ -325,8 +343,9 @@
             gmix[:, lanes(h)] = g
             st_own[1, h] = o
 
-    per_heads(turn)
-    scan_start(1)
+    for c in range(hq):
+        turn(chunk_heads(c))
+        scan_start(1, c)
 
     def intra_backward(hs):
         qs = [lq[:, lanes(h)] for h in hs]
@@ -344,8 +363,9 @@
             gk_acc[:, lanes(h)] = b
             gv_acc[:, lanes(h)] = c
 
-    per_heads(intra_backward)
-    scan_middle(1)
+    for c in range(hq):
+        intra_backward(chunk_heads(c))
+        scan_middle(1, c)
 
     def earlier_plane(k, _):
         kv_arrival(k).wait_recv()
@@ -356,9 +376,6 @@
 
         lax.fori_loop(0, G, one, 0)
         return 0
-
-    lax.fori_loop(1, z + 1, earlier_plane, 0)
-    scan_end(1)
 
     def finish(b, _):
         out = acc[b] / total[b]
@@ -367,8 +384,6 @@
                 out[:, h * length : (h + 1) * length]
             ).astype(bf16)
         return 0
-
-    lax.fori_loop(0, G, finish, 0)
 
     def out_copies():
         return [
@@ -379,10 +394,21 @@
             for d in range(1, G)
         ]
 
-    for copy in out_copies():
-        copy.start()
-    soft_out[:, pl.ds(pl.multiple_of(p * qw, HD), qw)] = o_own[p]
-    scan_done(1)
+    for copy in soft_copies((3,)):
+        copy.wait_recv()
+
+    def soft_rest():
+        lax.fori_loop(0, G, own_tile, 0)
+        lax.fori_loop(1, z + 1, earlier_plane, 0)
+        lax.fori_loop(0, G, finish, 0)
+        for copy in out_copies():
+            copy.start()
+        soft_out[:, pl.ds(pl.multiple_of(p * qw, HD), qw)] = o_own[p]
+
+    pl.when(z < planes // 2)(soft_rest)
+    for c in range(hq):
+        scan_end(1, c)
+    pl.when(z >= planes // 2)(soft_rest)
 
     def inter_backward(hs):
         ks = [lk[:, lanes(h)] for h in hs]
@@ -394,13 +420,17 @@
             grad_k[:, lanes(h)] = a.astype(bf16)
             grad_v[:, lanes(h)] = b.astype(bf16)
 
-    per_heads(inter_backward)
+    for c in range(hq):
+        scan_done(1, c)
+        inter_backward(chunk_heads(c))
 
     for copy in out_copies():
         copy.wait_recv()
-    for copy in scan_a(0) + scan_a(1) + scan_c(0) + scan_c(1):
-        copy.wait_send()
-    for copy in soft_copies() + exchange() + out_copies():
+    for way in (0, 1):
+        for c in range(hq):
+            for copy in scan_a(way, c) + scan_c(way, c):
+                copy.wait_send()
+    for copy in soft_copies((0, 1, 2, 3)) + exchange() + out_copies():
         copy.wait_send()
     for k in range(1, planes):
 
@@ -412,7 +442,8 @@
 
             @pl.when(sends_z(way, k))
             def _():
-                scan_z(way, k).wait_send()
+                for c in range(hq):
+                    scan_z(way, k, c).wait_send()
 
 
 def on_device(n, n_tp, lq, lk, lv, lg, sq, sk, sv, doc_start):
@@ -422,12 +453,18 @@
     planes = n // G
     q_width = sq.shape[1]
     qw = q_width // G
-    doc = jnp.broadcast_to(doc_start[None, :], (8, length))
+    doc_row = doc_start.reshape(1, length)
     dma = pltpu.SemaphoreType.DMA
     vm = pltpu.VMEM
     span = G * length
     others = planes - 1
+    kv_width = sk.shape[1]
     scratch = [
+        vm((length, width), bf16), vm((length, width), bf16),
+        vm((length, width), bf16), vm((length, width), bf16),
+        vm((length, q_width), bf16), vm((length, kv_width), bf16), vm((length, kv_width), bf16),
+        vm((8, length), jnp.int32),
+        dma((7,)),
         vm((2, heads, HD, HD), bf16),
         vm((2, G, hq, HD, HD), bf16),
         vm((2, hq, HD, HD), bf16),
@@ -449,25 +486,44 @@
         vm((G, 1, qw), f32),
         vm((G, 1, qw), f32),
         vm((G, HD, qw), f32),
-        dma((2, G - 1)), dma((2, G - 1)),
-        dma((2, others)), dma((2, others)),
-        dma((2, G - 1)), dma((2, G - 1)),
+        vm((HD, HD), f32),
+        dma((2, G - 1, hq)), dma((2, G - 1, hq)),
+        dma((2, others, hq)), dma((2, others, hq)),
+        dma((2, G - 1, hq)), dma((2, G - 1, hq)),
         dma((n_tp - 1,)), dma((n_tp - 1,)),
         dma((G - 1, 4)), dma((G - 1, 4)),
         dma((others,)), dma((others,)),
         dma((G - 1,)), dma((G - 1,)),
     ]
-    shape = jax.ShapeDtypeStruct((length, width), bf16)
-    return pl.pallas_call(
+    hbm = pl.BlockSpec(memory_space=pl.ANY)
+    here = pl.BlockSpec(memory_space=pltpu.VMEM)
+    widths = [width] * 4 + [q_width]
+    held = pl.pallas_call(
         functools.partial(kernel, n, n_tp),
-        out_shape=[shape] * 4 + [jax.ShapeDtypeStruct((length, q_width), bf16)],
-        in_specs=[pl.BlockSpec(memory_space=pltpu.VMEM)] * 8,
-        out_specs=[pl.BlockSpec(memory_space=pltpu.VMEM)] * 5,
+        out_shape=[pltpu.VMEM((length, w), bf16) for w in widths],
+        in_specs=[hbm] * 7 + [here],
+        out_specs=[here] * 5,
         scratch_shapes=scratch,
         compiler_params=pltpu.CompilerParams(
-            collective_id=0, has_side_effects=True, vmem_limit_bytes=48 * 1024 * 1024
+            collective_id=0, has_side_effects=True, vmem_limit_bytes=52 * 1024 * 1024
         ),
-    )(lq, lk, lv, lg, sq, sk, sv, doc)
+    )(lq, lk, lv, lg, sq, sk, sv, doc_row)
+    return pl.pallas_call(
+        write_out,
+        out_shape=[jax.ShapeDtypeStruct((length, w), bf16) for w in widths],
+        in_specs=[here] * 5,
+        out_specs=[hbm] * 5,
+        scratch_shapes=[dma((5,))],
+    )(*held)
+
+
+def write_out(*refs):
+    sems = refs[10]
+    copies = [pltpu.make_async_copy(refs[i], refs[5 + i], sems.at[i]) for i in range(5)]
+    for copy in copies:
+        copy.start()
+    for copy in copies:
+        copy.wait()
 
 
 def solution(mesh):

time: 81.2 us -> 65 us (0.80)
  the two profiles are of different devices: /device:TPU:0 before, /device:TPU:17 now
where the time goes in v2:
time: 65 us; the launch traced here: 64.8 us
  Pallas kernels  60.2 us (93%)
  local copies, waits for them, and re-layouts  3.95 us (6%)
  between operations  0.65 us (1%)
    pallas_call x1, Pallas kernels, on_device(): pl.pallas_call(functools.partial(kernel, n, n_tp), out_shape=[pltpu.VMEM(...  57 us
    unnamed x10, local copies, waits for them, and re-layouts  3.95 us
    pallas_call x1, Pallas kernels, on_device(): pl.pallas_call(write_out, out_shape=[jax.ShapeDtypeStruct((length, w), bf...  3.2 us

profile of v2, /device:TPU:17, one launch (start us, length us, event | category | flops | bytes accessed | tf_op | source)
XLA Modules:
  0.0 64.8 jit_solution(4605954064067512525)
XLA Ops:
  0.6 57.0 %shard_map.119 = (bf16[128,2048]{1,0:T(8,128)(2,1)S(1)}, bf16[128,2048]{1,0:T(8,128)(2,1)S(1)}, bf16[128,2048]{1,0:T(8,128)(2,1)S(1)}, bf16[128,2048]{1,0:T(8,128)(2,1)S(1)}, bf16[128,2048]{1,0:T(8,128)(2,1)S(1)}) custom-call(bf16[128,2048]{1,0:T(8,128)(2,1)} %lq_hbm.1, bf16[128,2048]{1,0:T(8,128)(2,1)} %lk_hbm.1, bf16[128,2048]{1,0:T(8,128)(2,1)} %lv_hbm.1, ...), custom_call_target="tpu_custom_call" | custom-call | tf_op jit(solution)/shard_map/pallas_call | solution.py:501
  57.7 0.0 copy-start
  57.7 0.8 %copy-done = bf16[128,2048]{1,0:T(8,128)(2,1)} copy-done((bf16[128,2048]{1,0:T(8,128)(2,1)}, bf16[128,2048]{1,0:T(8,128)(2,1)S(1)}, u32[]{:S(2)}) %copy-start) | copy-done | bytes 524312
  58.5 0.0 copy-start.1
  58.5 0.8 %copy-done.1 = bf16[128,2048]{1,0:T(8,128)(2,1)} copy-done((bf16[128,2048]{1,0:T(8,128)(2,1)}, bf16[128,2048]{1,0:T(8,128)(2,1)S(1)}, u32[]{:S(2)}) %copy-start.1) | copy-done | bytes 524312
  59.3 0.0 copy-start.2
  59.3 0.8 %copy-done.2 = bf16[128,2048]{1,0:T(8,128)(2,1)} copy-done((bf16[128,2048]{1,0:T(8,128)(2,1)}, bf16[128,2048]{1,0:T(8,128)(2,1)S(1)}, u32[]{:S(2)}) %copy-start.2) | copy-done | bytes 524312
  60.1 0.0 copy-start.3
  60.1 0.8 %copy-done.3 = bf16[128,2048]{1,0:T(8,128)(2,1)} copy-done((bf16[128,2048]{1,0:T(8,128)(2,1)}, bf16[128,2048]{1,0:T(8,128)(2,1)S(1)}, u32[]{:S(2)}) %copy-start.3) | copy-done | bytes 524312
  60.9 0.0 copy-start.4
  60.9 0.8 %copy-done.4 = bf16[128,2048]{1,0:T(8,128)(2,1)} copy-done((bf16[128,2048]{1,0:T(8,128)(2,1)}, bf16[128,2048]{1,0:T(8,128)(2,1)S(1)}, u32[]{:S(2)}) %copy-start.4) | copy-done | bytes 524312
  61.6 3.2 %shard_map.120 = (bf16[128,2048]{1,0:T(8,128)(2,1)}, bf16[128,2048]{1,0:T(8,128)(2,1)}, bf16[128,2048]{1,0:T(8,128)(2,1)}, bf16[128,2048]{1,0:T(8,128)(2,1)}, bf16[128,2048]{1,0:T(8,128)(2,1)}) custom-call(bf16[128,2048]{1,0:T(8,128)(2,1)} %copy-done, bf16[128,2048]{1,0:T(8,128)(2,1)} %copy-done.1, bf16[128,2048]{1,0:T(8,128)(2,1)} %copy-done.2, ...), custom_call_target="tpu_custom_call" | custom-call | tf_op jit(solution)/shard_map/pallas_call | solution.py:511
Async XLA Ops:
  57.7 0.8 %copy-start = (bf16[128,2048]{1,0:T(8,128)(2,1)}, bf16[128,2048]{1,0:T(8,128)(2,1)S(1)}, u32[]{:S(2)}) copy-start(bf16[128,2048]{1,0:T(8,128)(2,1)S(1)} %get-tuple-element.10.refs_0_) | copy-start | bytes 1572868
  58.5 0.8 %copy-start.1 = (bf16[128,2048]{1,0:T(8,128)(2,1)}, bf16[128,2048]{1,0:T(8,128)(2,1)S(1)}, u32[]{:S(2)}) copy-start(bf16[128,2048]{1,0:T(8,128)(2,1)S(1)} %get-tuple-element.11.refs_1_) | copy-start | bytes 1572868
  59.3 0.8 %copy-start.2 = (bf16[128,2048]{1,0:T(8,128)(2,1)}, bf16[128,2048]{1,0:T(8,128)(2,1)S(1)}, u32[]{:S(2)}) copy-start(bf16[128,2048]{1,0:T(8,128)(2,1)S(1)} %get-tuple-element.12.refs_2_) | copy-start | bytes 1572868
  60.1 0.8 %copy-start.3 = (bf16[128,2048]{1,0:T(8,128)(2,1)}, bf16[128,2048]{1,0:T(8,128)(2,1)S(1)}, u32[]{:S(2)}) copy-start(bf16[128,2048]{1,0:T(8,128)(2,1)S(1)} %get-tuple-element.13.refs_3_) | copy-start | bytes 1572868
  60.9 0.8 %copy-start.4 = (bf16[128,2048]{1,0:T(8,128)(2,1)}, bf16[128,2048]{1,0:T(8,128)(2,1)S(1)}, u32[]{:S(2)}) copy-start(bf16[128,2048]{1,0:T(8,128)(2,1)S(1)} %get-tuple-element.14.refs_4_) | copy-start | bytes 1572868

commit v3 on v2

--- a/solution.py
+++ b/solution.py
@@ -230,8 +230,6 @@
         if c == (hq - 1) // 2:
             for copy in soft_copies((0, 1, 2)):
                 copy.start()
-    for copy in soft_copies((3,)):
-        copy.start()
     for copy in soft_copies((0, 1, 2)):
         copy.wait_recv()
 
@@ -254,42 +252,77 @@
     span = G * length
     factor = math.log2(math.e) / math.sqrt(HD)
 
-    def tile(b, zz, first):
-        keys = kv[zz, 0]
-        vals = kv[zz, 1]
-        raw = dot(keys, q_rows[b], 1, 1) * factor
-        key_pos = zz * span + lax.broadcasted_iota(jnp.int32, (span, qw), 0)
+    def tile(b, zz, first, count):
+        keys = kv[zz, 0, :count]
+        vals = kv[zz, 1, :count]
+        raw = dot(keys, q_rows[...], 1, 1) * factor
+        row = lax.broadcasted_iota(jnp.int32, (count, qw), 0)
         begins = jnp.concatenate([doc_in[b][0:1, :]] * mine, axis=1)
-        allowed = key_pos >= begins
+        allowed = row >= begins - zz * span
         if first:
             one = lax.broadcasted_iota(jnp.int32, (1, length), 1)
-            q_pos = z * span + b * length + jnp.concatenate([one] * mine, axis=1)
-            allowed = allowed & (key_pos <= q_pos)
+            allowed = allowed & (row <= b * length + jnp.concatenate([one] * mine, axis=1))
         raw = jnp.where(allowed, raw, floor_score)
         high = jnp.max(raw, axis=0, keepdims=True)
         if not first:
-            old = top[b]
+            old = top[...]
             high = jnp.maximum(old, high)
             shrink = jnp.exp2(old - high)
         probs = jnp.exp2(raw - high)
         summed = jnp.sum(probs, axis=0, keepdims=True)
         update = dot(vals, probs.astype(bf16), 0, 0)
-        top[b] = high
+        top[...] = high
         if first:
-            total[b] = summed
-            acc[b] = update
+            total[...] = summed
+            acc[...] = update
         else:
-            total[b] = total[b] * shrink + summed
-            acc[b] = acc[b] * shrink + update
-
-    def own_tile(b, _):
+            total[...] = total[...] * shrink + summed
+            acc[...] = acc[...] * shrink + update
+
+    def out_copy(b, d):
+        return remote(
+            o_own.at[b], soft_out.at[:, pl.ds(pl.multiple_of(p * qw, HD), qw)],
+            o_send.at[d], o_recv.at[d], at_member(b),
+        )
+
+    def query_block(i, _):
+        b = member(i + 1)
         for h in range(mine):
-            q_rows[b, h * length : (h + 1) * length, :] = q_in[b, :, h * HD : (h + 1) * HD]
-        tile(b, z, True)
+            q_rows[h * length : (h + 1) * length, :] = q_in[b, :, h * HD : (h + 1) * HD]
+
+        @pl.when(b < G // 2)
+        def _():
+            tile(b, z, True, span // 2)
+
+        @pl.when(b >= G // 2)
+        def _():
+            tile(b, z, True, span)
+
+        def earlier_plane(k, _):
+            @pl.when(i == 0)
+            def _():
+                kv_arrival(k).wait_recv()
+
+            tile(b, z - k, False, span)
+            return 0
+
+        lax.fori_loop(1, z + 1, earlier_plane, 0)
+        out = acc[...] / total[...]
+        for h in range(mine):
+            o_own[b, :, h * HD : (h + 1) * HD] = jnp.transpose(
+                out[:, h * length : (h + 1) * length]
+            ).astype(bf16)
+
+        @pl.when(i < G - 1)
+        def _():
+            out_copy(b, i).start()
+
         return 0
 
     for c in range(hq):
         scan_end(0, c)
+    for copy in soft_copies((3,)):
+        copy.start()
     loads[6].wait()
 
     ex_own[...] = jnp.zeros_like(ex_own)
@@ -367,48 +400,14 @@
         intra_backward(chunk_heads(c))
         scan_middle(1, c)
 
-    def earlier_plane(k, _):
-        kv_arrival(k).wait_recv()
-
-        def one(b, _):
-            tile(b, z - k, False)
-            return 0
-
-        lax.fori_loop(0, G, one, 0)
-        return 0
-
-    def finish(b, _):
-        out = acc[b] / total[b]
-        for h in range(mine):
-            o_own[b, :, h * HD : (h + 1) * HD] = jnp.transpose(
-                out[:, h * length : (h + 1) * length]
-            ).astype(bf16)
-        return 0
-
-    def out_copies():
-        return [
-            remote(
-                o_own.at[member(d)], soft_out.at[:, pl.ds(pl.multiple_of(p * qw, HD), qw)],
-                o_send.at[d - 1], o_recv.at[d - 1], at_member(member(d)),
-            )
-            for d in range(1, G)
-        ]
-
     for copy in soft_copies((3,)):
         copy.wait_recv()
-
-    def soft_rest():
-        lax.fori_loop(0, G, own_tile, 0)
-        lax.fori_loop(1, z + 1, earlier_plane, 0)
-        lax.fori_loop(0, G, finish, 0)
-        for copy in out_copies():
-            copy.start()
-        soft_out[:, pl.ds(pl.multiple_of(p * qw, HD), qw)] = o_own[p]
-
-    pl.when(z < planes // 2)(soft_rest)
+    ahead = jnp.where(z < planes // 2, G, jnp.where(z < planes - 1, 1, 0))
+    lax.fori_loop(0, ahead, query_block, 0)
     for c in range(hq):
         scan_end(1, c)
-    pl.when(z >= planes // 2)(soft_rest)
+    lax.fori_loop(ahead, G, query_block, 0)
+    soft_out[:, pl.ds(pl.multiple_of(p * qw, HD), qw)] = o_own[p]
 
     def inter_backward(hs):
         ks = [lk[:, lanes(h)] for h in hs]
@@ -424,13 +423,14 @@
         scan_done(1, c)
         inter_backward(chunk_heads(c))
 
-    for copy in out_copies():
+    out_copies = [out_copy(member(d + 1), d) for d in range(G - 1)]
+    for copy in out_copies:
         copy.wait_recv()
     for way in (0, 1):
         for c in range(hq):
             for copy in scan_a(way, c) + scan_c(way, c):
                 copy.wait_send()
-    for copy in soft_copies((0, 1, 2, 3)) + exchange() + out_copies():
+    for copy in soft_copies((0, 1, 2, 3)) + exchange() + out_copies:
         copy.wait_send()
     for k in range(1, planes):
 
@@ -480,12 +480,12 @@
         vm((n_tp - 1, 2, length, HD), f32),
         vm((planes, 2, span, HD), bf16),
         vm((G, length, qw), bf16),
-        vm((G, qw // HD * length, HD), bf16),
+        vm((qw // HD * length, HD), bf16),
         vm((G, 8, length), jnp.int32),
         vm((G, length, qw), bf16),
-        vm((G, 1, qw), f32),
-        vm((G, 1, qw), f32),
-        vm((G, HD, qw), f32),
+        vm((1, qw), f32),
+        vm((1, qw), f32),
+        vm((HD, qw), f32),
         vm((HD, HD), f32),
         dma((2, G - 1, hq)), dma((2, G - 1, hq)),
         dma((2, others, hq)), dma((2, others, hq)),
@@ -514,6 +514,7 @@
         in_specs=[here] * 5,
         out_specs=[hbm] * 5,
         scratch_shapes=[dma((5,))],
+        compiler_params=pltpu.CompilerParams(vmem_limit_bytes=8 * 1024 * 1024),
     )(*held)
 
 

time: 65 us -> 56.7 us (0.87)
  the two profiles are of different devices: /device:TPU:17 before, /device:TPU:26 now
where the time goes in v3:
time: 56.7 us; the launch traced here: 56.6 us
  Pallas kernels  55.9 us (99%)
  between operations  0.64 us (1%)
    pallas_call x1, Pallas kernels, on_device(): pl.pallas_call(functools.partial(kernel, n, n_tp), out_shape=[pltpu.VMEM(...  54.4 us
    pallas_call x1, Pallas kernels, on_device(): pl.pallas_call(write_out, out_shape=[jax.ShapeDtypeStruct((length, w), bf...  1.53 us

profile of v3, /device:TPU:26, one launch (start us, length us, event | category | flops | bytes accessed | tf_op | source)
XLA Modules:
  0.0 56.6 jit_solution(6933107860794664422)
XLA Ops:
  0.6 54.4 %shard_map.119 = (bf16[128,2048]{1,0:T(8,128)(2,1)S(1)}, bf16[128,2048]{1,0:T(8,128)(2,1)S(1)}, bf16[128,2048]{1,0:T(8,128)(2,1)S(1)}, bf16[128,2048]{1,0:T(8,128)(2,1)S(1)}, bf16[128,2048]{1,0:T(8,128)(2,1)S(1)}) custom-call(bf16[128,2048]{1,0:T(8,128)(2,1)} %lq_hbm.1, bf16[128,2048]{1,0:T(8,128)(2,1)} %lk_hbm.1, bf16[128,2048]{1,0:T(8,128)(2,1)} %lv_hbm.1, ...), custom_call_target="tpu_custom_call" | custom-call | tf_op jit(solution)/shard_map/pallas_call | solution.py:501
  55.0 1.5 %shard_map.120 = (bf16[128,2048]{1,0:T(8,128)(2,1)}, bf16[128,2048]{1,0:T(8,128)(2,1)}, bf16[128,2048]{1,0:T(8,128)(2,1)}, bf16[128,2048]{1,0:T(8,128)(2,1)}, bf16[128,2048]{1,0:T(8,128)(2,1)}) custom-call(bf16[128,2048]{1,0:T(8,128)(2,1)S(1)} %get-tuple-element.10.refs_0_, bf16[128,2048]{1,0:T(8,128)(2,1)S(1)} %get-tuple-element.11.refs_1_, ...), custom_call_target="tpu_custom_call" | custom-call | tf_op jit(solution)/shard_map/pallas_call | solution.py:511

commit v4 on v3

--- a/solution.py
+++ b/solution.py
@@ -31,7 +31,7 @@
     st_own, st_in, st_tot, st_z, st_out, st_fin,
     scores, mix, gmix, gk_acc, gv_acc,
     ex_own, ex_in,
-    kv, q_in, q_rows, doc_in, o_own, top, total, acc, carry_ref,
+    kv, q_in, q_rows, doc_in, o_own, top, total, acc, carry_ref, st_sum,
     a_send, a_recv, z_send, z_recv, c_send, c_recv,
     e_send, e_recv, s_send, s_recv, kvz_send, kvz_recv, o_send, o_recv,
 ):
@@ -77,10 +77,14 @@
     barrier = pltpu.get_barrier_semaphore()
     for d in range(1, G):
         pl.semaphore_signal(barrier, inc=1, device_id=at_member(member(d)), device_id_type=MESH)
-    for k in range(1, planes):
-        pl.semaphore_signal(
-            barrier, inc=1, device_id=at_plane(lax.rem(z + k, planes)), device_id_type=MESH
-        )
+    for step, there in ((1, z + 1 < planes), (-1, z > 0)):
+
+        @pl.when(there)
+        def _():
+            pl.semaphore_signal(
+                barrier, inc=1, device_id=at_plane(z + step), device_id_type=MESH
+            )
+
     for k in range(1, n_tp):
         pl.semaphore_signal(
             barrier, inc=1, device_id={"tp": lax.rem(tp + k, n_tp)}, device_id_type=MESH
@@ -112,15 +116,17 @@
             for d in range(1, G)
         ]
 
-    def scan_z(way, k, c):
-        there = z - k if way else z + k
+    def scan_z(way, c):
         return remote(
-            st_tot.at[way, c], st_z.at[way, k - 1, c],
-            z_send.at[way, k - 1, c], z_recv.at[way, k - 1, c], at_plane(there),
+            st_tot.at[way, c], st_z.at[way, c], z_send.at[way, c], z_recv.at[way, c],
+            at_plane(z - 1 if way else z + 1),
         )
 
-    def sends_z(way, k):
-        return (z - k >= 0) if way else (z + k < planes)
+    def passes_on(way):
+        return z > 0 if way else z + 1 < planes
+
+    def is_passed(way):
+        return passes_on(1 - way)
 
     def scan_c(way, c):
         return [
@@ -140,21 +146,25 @@
         for copy in scan_a(way, c):
             copy.wait_recv()
         parts = [st_in[way, s, c].astype(f32) for s in range(G)]
-        st_tot[way, c] = ((parts[0] + parts[1]) + (parts[2] + parts[3])).astype(bf16)
-        for k in range(1, planes):
-
-            @pl.when(sends_z(way, k))
-            def _():
-                scan_z(way, k, c).start()
+        st_sum[c] = (parts[0] + parts[1]) + (parts[2] + parts[3])
+
+        @pl.when(passes_on(way) & jnp.logical_not(is_passed(way)))
+        def _():
+            st_tot[way, c] = st_sum[c].astype(bf16)
+            scan_z(way, c).start()
 
     def scan_end(way, c):
         carry_ref[...] = jnp.zeros((HD, HD), f32)
-        for k in range(1, planes):
-
-            @pl.when(sends_z(1 - way, k))
-            def _():
-                scan_z(way, k, c).wait_recv()
-                carry_ref[...] += st_z[way, k - 1, c].astype(f32)
+
+        @pl.when(is_passed(way))
+        def _():
+            scan_z(way, c).wait_recv()
+            carry_ref[...] = st_z[way, c].astype(f32)
+
+        @pl.when(is_passed(way) & passes_on(way))
+        def _():
+            st_tot[way, c] = (carry_ref[...] + st_sum[c]).astype(bf16)
+            scan_z(way, c).start()
 
         carry = carry_ref[...]
         order = range(G - 1, -1, -1) if way else range(G)
@@ -178,7 +188,8 @@
         for h, o in zip(hs, outs):
             st_own[0, h] = o
         if c == 0:
-            pl.semaphore_wait(barrier, (G - 1) + (planes - 1) + (n_tp - 1))
+            near = jnp.where(z + 1 < planes, 1, 0) + jnp.where(z > 0, 1, 0)
+            pl.semaphore_wait(barrier, (G - 1) + (n_tp - 1) + near)
         scan_start(0, c)
 
     def kv_lanes(r):
@@ -224,30 +235,37 @@
             scores[h] = w
             mix[:, lanes(h)] = m
 
+    last = z == planes - 1
+
+    def soft_start(which):
+        for copy in soft_copies(which):
+            copy.start()
+
+    pl.when(last)(lambda: soft_start((3,)))
+    pl.when(jnp.logical_not(last))(lambda: soft_start((0, 1, 2)))
     for c in range(hq):
         intra_forward(chunk_heads(c))
-        scan_middle(0, c)
-        if c == (hq - 1) // 2:
-            for copy in soft_copies((0, 1, 2)):
-                copy.start()
-    for copy in soft_copies((0, 1, 2)):
-        copy.wait_recv()
-
-    def kv_copy(k):
-        return remote(
-            kv.at[z], kv.at[z], kvz_send.at[k - 1], kvz_recv.at[k - 1], at_plane(z + k)
-        )
+
+    def kv_hop(k):
+        block = kv.at[z - k + 1]
+        return remote(block, block, kvz_send.at[k - 1], kvz_recv.at[k - 1], at_plane(z + 1))
 
     def kv_arrival(k):
-        return remote(
-            kv.at[z - k], kv.at[z - k], kvz_send.at[k - 1], kvz_recv.at[k - 1], at_plane(z - k)
-        )
-
-    for k in range(1, planes):
-
-        @pl.when(z + k < planes)
-        def _():
-            kv_copy(k).start()
+        block = kv.at[z - k]
+        return remote(block, block, kvz_send.at[k - 1], kvz_recv.at[k - 1], at_plane(z - 1))
+
+    def hops(k):
+        return (z + 1 < planes) & (z - k + 1 >= 0)
+
+    def kv_pass(k):
+        @pl.when(hops(k))
+        def _():
+            if k == 1:
+                for copy in soft_copies((0, 1, 2)):
+                    copy.wait_recv()
+            else:
+                kv_arrival(k - 1).wait_recv()
+            kv_hop(k).start()
 
     span = G * length
     factor = math.log2(math.e) / math.sqrt(HD)
@@ -299,7 +317,7 @@
             tile(b, z, True, span)
 
         def earlier_plane(k, _):
-            @pl.when(i == 0)
+            @pl.when((i == 0) & jnp.logical_not(hops(k + 1)))
             def _():
                 kv_arrival(k).wait_recv()
 
@@ -320,9 +338,11 @@
         return 0
 
     for c in range(hq):
+        scan_middle(0, c)
         scan_end(0, c)
-    for copy in soft_copies((3,)):
-        copy.start()
+    pl.when(last)(lambda: soft_start((0, 1, 2)))
+    pl.when(jnp.logical_not(last))(lambda: soft_start((3,)))
+    kv_pass(1)
     loads[6].wait()
 
     ex_own[...] = jnp.zeros_like(ex_own)
@@ -356,6 +376,8 @@
 
     for copy in exchange():
         copy.start()
+    if planes > 2:
+        kv_pass(2)
     for copy in exchange():
         copy.wait_recv()
     square, inner = ex_own[0], ex_own[1]
@@ -379,6 +401,8 @@
     for c in range(hq):
         turn(chunk_heads(c))
         scan_start(1, c)
+    for k in range(3, planes):
+        kv_pass(k)
 
     def intra_backward(hs):
         qs = [lq[:, lanes(h)] for h in hs]
@@ -402,7 +426,13 @@
 
     for copy in soft_copies((3,)):
         copy.wait_recv()
-    ahead = jnp.where(z < planes // 2, G, jnp.where(z < planes - 1, 1, 0))
+
+    @pl.when(last)
+    def _():
+        for copy in soft_copies((0, 1, 2)):
+            copy.wait_recv()
+
+    ahead = jnp.where(z < planes // 2, G, jnp.where(last, 0, 1))
     lax.fori_loop(0, ahead, query_block, 0)
     for c in range(hq):
         scan_end(1, c)
@@ -434,16 +464,16 @@
         copy.wait_send()
     for k in range(1, planes):
 
-        @pl.when(z + k < planes)
-        def _():
-            kv_copy(k).wait_send()
-
-        for way in (0, 1):
-
-            @pl.when(sends_z(way, k))
-            def _():
-                for c in range(hq):
-                    scan_z(way, k, c).wait_send()
+        @pl.when(hops(k))
+        def _():
+            kv_hop(k).wait_send()
+
+    for way in (0, 1):
+
+        @pl.when(passes_on(way))
+        def _():
+            for c in range(hq):
+                scan_z(way, c).wait_send()
 
 
 def on_device(n, n_tp, lq, lk, lv, lg, sq, sk, sv, doc_start):
@@ -468,7 +498,7 @@
         vm((2, heads, HD, HD), bf16),
         vm((2, G, hq, HD, HD), bf16),
         vm((2, hq, HD, HD), bf16),
-        vm((2, others, hq, HD, HD), bf16),
+        vm((2, hq, HD, HD), bf16),
         vm((2, G, hq, HD, HD), bf16),
         vm((2, heads, HD, HD), bf16),
         vm((heads, length, length), bf16),
@@ -487,8 +517,9 @@
         vm((1, qw), f32),
         vm((HD, qw), f32),
         vm((HD, HD), f32),
+        vm((hq, HD, HD), f32),
         dma((2, G - 1, hq)), dma((2, G - 1, hq)),
-        dma((2, others, hq)), dma((2, others, hq)),
+        dma((2, hq)), dma((2, hq)),
         dma((2, G - 1, hq)), dma((2, G - 1, hq)),
         dma((n_tp - 1,)), dma((n_tp - 1,)),
         dma((G - 1, 4)), dma((G - 1, 4)),

time: 56.7 us -> 52.2 us (0.921)
  the two profiles are of different devices: /device:TPU:26 before, /device:TPU:0 now
where the time goes in v4:
time: 52.2 us; the launch traced here: 52 us
  Pallas kernels  51.4 us (98%)
  between operations  0.64 us (1%)
    pallas_call x1, Pallas kernels, on_device(): pl.pallas_call(functools.partial(kernel, n, n_tp), out_shape=[pltpu.VMEM(...  49.9 us
    pallas_call x1, Pallas kernels, on_device(): pl.pallas_call(write_out, out_shape=[jax.ShapeDtypeStruct((length, w), bf...  1.53 us

profile of v4, /device:TPU:0, one launch (start us, length us, event | category | flops | bytes accessed | tf_op | source)
XLA Modules:
  0.0 52.0 jit_solution(1701954988471571773)
XLA Ops:
  0.6 49.9 %shard_map.119 = (bf16[128,2048]{1,0:T(8,128)(2,1)S(1)}, bf16[128,2048]{1,0:T(8,128)(2,1)S(1)}, bf16[128,2048]{1,0:T(8,128)(2,1)S(1)}, bf16[128,2048]{1,0:T(8,128)(2,1)S(1)}, bf16[128,2048]{1,0:T(8,128)(2,1)S(1)}) custom-call(bf16[128,2048]{1,0:T(8,128)(2,1)} %lq_hbm.1, bf16[128,2048]{1,0:T(8,128)(2,1)} %lk_hbm.1, bf16[128,2048]{1,0:T(8,128)(2,1)} %lv_hbm.1, ...), custom_call_target="tpu_custom_call" | custom-call | tf_op jit(solution)/shard_map/pallas_call | solution.py:532
  50.5 1.5 %shard_map.120 = (bf16[128,2048]{1,0:T(8,128)(2,1)}, bf16[128,2048]{1,0:T(8,128)(2,1)}, bf16[128,2048]{1,0:T(8,128)(2,1)}, bf16[128,2048]{1,0:T(8,128)(2,1)}, bf16[128,2048]{1,0:T(8,128)(2,1)}) custom-call(bf16[128,2048]{1,0:T(8,128)(2,1)S(1)} %get-tuple-element.10.refs_0_, bf16[128,2048]{1,0:T(8,128)(2,1)S(1)} %get-tuple-element.11.refs_1_, ...), custom_call_target="tpu_custom_call" | custom-call | tf_op jit(solution)/shard_map/pallas_call | solution.py:542

commit v5 on v4

--- a/solution.py
+++ b/solution.py
@@ -50,6 +50,7 @@
     heads = lq.shape[1] // HD
     hq = heads // G
     planes = n // G
+    levels = planes.bit_length() - 1
     q_heads = sq.shape[1] // HD
     kv_heads = sk.shape[1] // HD
     mine = q_heads // G
@@ -77,14 +78,10 @@
     barrier = pltpu.get_barrier_semaphore()
     for d in range(1, G):
         pl.semaphore_signal(barrier, inc=1, device_id=at_member(member(d)), device_id_type=MESH)
-    for step, there in ((1, z + 1 < planes), (-1, z > 0)):
-
-        @pl.when(there)
-        def _():
-            pl.semaphore_signal(
-                barrier, inc=1, device_id=at_plane(z + step), device_id_type=MESH
-            )
-
+    for k in range(1, planes):
+        pl.semaphore_signal(
+            barrier, inc=1, device_id=at_plane(lax.rem(z + k, planes)), device_id_type=MESH
+        )
     for k in range(1, n_tp):
         pl.semaphore_signal(
             barrier, inc=1, device_id={"tp": lax.rem(tp + k, n_tp)}, device_id_type=MESH
@@ -116,17 +113,30 @@
             for d in range(1, G)
         ]
 
-    def scan_z(way, c):
+    def place(way):
+        return planes - 1 - z if way else z
+
+    def scan_z(way, level, j, c):
         return remote(
-            st_tot.at[way, c], st_z.at[way, c], z_send.at[way, c], z_recv.at[way, c],
-            at_plane(z - 1 if way else z + 1),
+            st_tot.at[way, c], st_z.at[way, level, c],
+            z_send.at[way, j, c], z_recv.at[way, level, c],
+            at_plane(z - 1 - j if way else z + 1 + j),
         )
 
-    def passes_on(way):
-        return z > 0 if way else z + 1 < planes
-
-    def is_passed(way):
-        return passes_on(1 - way)
+    def gives(way, level):
+        half = 1 << level
+        return lax.rem(place(way), 2 * half) == half - 1
+
+    def takes(way, level):
+        half = 1 << level
+        return lax.rem(place(way), 2 * half) >= half
+
+    def scan_give(way, level, c, value):
+        @pl.when(gives(way, level))
+        def _():
+            st_tot[way, c] = value().astype(bf16)
+            for j in range(1 << level):
+                scan_z(way, level, j, c).start()
 
     def scan_c(way, c):
         return [
@@ -148,23 +158,19 @@
         parts = [st_in[way, s, c].astype(f32) for s in range(G)]
         st_sum[c] = (parts[0] + parts[1]) + (parts[2] + parts[3])
 
-        @pl.when(passes_on(way) & jnp.logical_not(is_passed(way)))
-        def _():
-            st_tot[way, c] = st_sum[c].astype(bf16)
-            scan_z(way, c).start()
+        if levels:
+            scan_give(way, 0, c, lambda: st_sum[c])
 
     def scan_end(way, c):
         carry_ref[...] = jnp.zeros((HD, HD), f32)
-
-        @pl.when(is_passed(way))
-        def _():
-            scan_z(way, c).wait_recv()
-            carry_ref[...] = st_z[way, c].astype(f32)
-
-        @pl.when(is_passed(way) & passes_on(way))
-        def _():
-            st_tot[way, c] = (carry_ref[...] + st_sum[c]).astype(bf16)
-            scan_z(way, c).start()
+        for level in range(levels):
+            if level:
+                scan_give(way, level, c, lambda: carry_ref[...] + st_sum[c])
+
+            @pl.when(takes(way, level))
+            def _():
+                scan_z(way, level, 0, c).wait_recv()
+                carry_ref[...] += st_z[way, level, c].astype(f32)
 
         carry = carry_ref[...]
         order = range(G - 1, -1, -1) if way else range(G)
@@ -188,8 +194,7 @@
         for h, o in zip(hs, outs):
             st_own[0, h] = o
         if c == 0:
-            near = jnp.where(z + 1 < planes, 1, 0) + jnp.where(z > 0, 1, 0)
-            pl.semaphore_wait(barrier, (G - 1) + (n_tp - 1) + near)
+            pl.semaphore_wait(barrier, (G - 1) + (planes - 1) + (n_tp - 1))
         scan_start(0, c)
 
     def kv_lanes(r):
@@ -339,6 +344,7 @@
 
     for c in range(hq):
         scan_middle(0, c)
+    for c in range(hq):
         scan_end(0, c)
     pl.when(last)(lambda: soft_start((0, 1, 2)))
     pl.when(jnp.logical_not(last))(lambda: soft_start((3,)))
@@ -421,8 +427,11 @@
             gv_acc[:, lanes(h)] = c
 
     for c in range(hq):
+        if c % 2 == 0:
+            intra_backward(chunk_heads(c // 2))
+        scan_middle(1, c)
+    for c in range((hq + 1) // 2, hq):
         intra_backward(chunk_heads(c))
-        scan_middle(1, c)
 
     for copy in soft_copies((3,)):
         copy.wait_recv()
@@ -432,7 +441,7 @@
         for copy in soft_copies((0, 1, 2)):
             copy.wait_recv()
 
-    ahead = jnp.where(z < planes // 2, G, jnp.where(last, 0, 1))
+    ahead = jnp.where(z < planes // 2, G // 2, 0)
     lax.fori_loop(0, ahead, query_block, 0)
     for c in range(hq):
         scan_end(1, c)
@@ -470,10 +479,13 @@
 
     for way in (0, 1):
 
-        @pl.when(passes_on(way))
-        def _():
-            for c in range(hq):
-                scan_z(way, c).wait_send()
+        for level in range(levels):
+
+            @pl.when(gives(way, level))
+            def _():
+                for c in range(hq):
+                    for j in range(1 << level):
+                        scan_z(way, level, j, c).wait_send()
 
 
 def on_device(n, n_tp, lq, lk, lv, lg, sq, sk, sv, doc_start):
@@ -488,6 +500,7 @@
     vm = pltpu.VMEM
     span = G * length
     others = planes - 1
+    levels = planes.bit_length() - 1
     kv_width = sk.shape[1]
     scratch = [
         vm((length, width), bf16), vm((length, width), bf16),
@@ -498,7 +511,7 @@
         vm((2, heads, HD, HD), bf16),
         vm((2, G, hq, HD, HD), bf16),
         vm((2, hq, HD, HD), bf16),
-        vm((2, hq, HD, HD), bf16),
+        vm((2, levels, hq, HD, HD), bf16),
         vm((2, G, hq, HD, HD), bf16),
         vm((2, heads, HD, HD), bf16),
         vm((heads, length, length), bf16),
@@ -519,7 +532,7 @@
         vm((HD, HD), f32),
         vm((hq, HD, HD), f32),
         dma((2, G - 1, hq)), dma((2, G - 1, hq)),
-        dma((2, hq)), dma((2, hq)),
+        dma((2, planes // 2, hq)), dma((2, levels, hq)),
         dma((2, G - 1, hq)), dma((2, G - 1, hq)),
         dma((n_tp - 1,)), dma((n_tp - 1,)),
         dma((G - 1, 4)), dma((G - 1, 4)),

time: 52.2 us -> 53.9 us (1.033)
  Pallas kernels: 51.4 us -> 53.1 us
    pallas_call x1, Pallas kernels: 49.9 us -> 51.5 us  [on_device(): pl.pallas_call(functools.partial(kernel, n, n_tp), out_shape=[pltpu.VMEM(...]
where the time goes in v5:
time: 53.9 us; the launch traced here: 53.7 us
  Pallas kernels  53.1 us (99%)
  between operations  0.64 us (1%)
    pallas_call x1, Pallas kernels, on_device(): pl.pallas_call(functools.partial(kernel, n, n_tp), out_shape=[pltpu.VMEM(...  51.5 us
    pallas_call x1, Pallas kernels, on_device(): pl.pallas_call(write_out, out_shape=[jax.ShapeDtypeStruct((length, w), bf...  1.53 us

profile of v5, /device:TPU:0, one launch (start us, length us, event | category | flops | bytes accessed | tf_op | source)
XLA Modules:
  0.0 53.7 jit_solution(15126757495926977806)
XLA Ops:
  0.6 51.5 %shard_map.119 = (bf16[128,2048]{1,0:T(8,128)(2,1)S(1)}, bf16[128,2048]{1,0:T(8,128)(2,1)S(1)}, bf16[128,2048]{1,0:T(8,128)(2,1)S(1)}, bf16[128,2048]{1,0:T(8,128)(2,1)S(1)}, bf16[128,2048]{1,0:T(8,128)(2,1)S(1)}) custom-call(bf16[128,2048]{1,0:T(8,128)(2,1)} %lq_hbm.1, bf16[128,2048]{1,0:T(8,128)(2,1)} %lk_hbm.1, bf16[128,2048]{1,0:T(8,128)(2,1)} %lv_hbm.1, ...), custom_call_target="tpu_custom_call" | custom-call | tf_op jit(solution)/shard_map/pallas_call | solution.py:545
  52.2 1.5 %shard_map.120 = (bf16[128,2048]{1,0:T(8,128)(2,1)}, bf16[128,2048]{1,0:T(8,128)(2,1)}, bf16[128,2048]{1,0:T(8,128)(2,1)}, bf16[128,2048]{1,0:T(8,128)(2,1)}, bf16[128,2048]{1,0:T(8,128)(2,1)}) custom-call(bf16[128,2048]{1,0:T(8,128)(2,1)S(1)} %get-tuple-element.10.refs_0_, bf16[128,2048]{1,0:T(8,128)(2,1)S(1)} %get-tuple-element.11.refs_1_, ...), custom_call_target="tpu_custom_call" | custom-call | tf_op jit(solution)/shard_map/pallas_call | solution.py:555

commit v6 on v4

--- a/solution.py
+++ b/solution.py
@@ -77,14 +77,10 @@
     barrier = pltpu.get_barrier_semaphore()
     for d in range(1, G):
         pl.semaphore_signal(barrier, inc=1, device_id=at_member(member(d)), device_id_type=MESH)
-    for step, there in ((1, z + 1 < planes), (-1, z > 0)):
-
-        @pl.when(there)
-        def _():
-            pl.semaphore_signal(
-                barrier, inc=1, device_id=at_plane(z + step), device_id_type=MESH
-            )
-
+    for k in range(1, planes):
+        pl.semaphore_signal(
+            barrier, inc=1, device_id=at_plane(lax.rem(z + k, planes)), device_id_type=MESH
+        )
     for k in range(1, n_tp):
         pl.semaphore_signal(
             barrier, inc=1, device_id={"tp": lax.rem(tp + k, n_tp)}, device_id_type=MESH
@@ -188,8 +184,7 @@
         for h, o in zip(hs, outs):
             st_own[0, h] = o
         if c == 0:
-            near = jnp.where(z + 1 < planes, 1, 0) + jnp.where(z > 0, 1, 0)
-            pl.semaphore_wait(barrier, (G - 1) + (n_tp - 1) + near)
+            pl.semaphore_wait(barrier, (G - 1) + (planes - 1) + (n_tp - 1))
         scan_start(0, c)
 
     def kv_lanes(r):
@@ -246,26 +241,22 @@
     for c in range(hq):
         intra_forward(chunk_heads(c))
 
-    def kv_hop(k):
-        block = kv.at[z - k + 1]
-        return remote(block, block, kvz_send.at[k - 1], kvz_recv.at[k - 1], at_plane(z + 1))
+    def kv_copy(k):
+        return remote(
+            kv.at[z], kv.at[z], kvz_send.at[k - 1], kvz_recv.at[k - 1], at_plane(z + k)
+        )
 
     def kv_arrival(k):
         block = kv.at[z - k]
-        return remote(block, block, kvz_send.at[k - 1], kvz_recv.at[k - 1], at_plane(z - 1))
-
-    def hops(k):
-        return (z + 1 < planes) & (z - k + 1 >= 0)
+        return remote(block, block, kvz_send.at[k - 1], kvz_recv.at[k - 1], at_plane(z - k))
 
     def kv_pass(k):
-        @pl.when(hops(k))
+        @pl.when(z + k < planes)
         def _():
             if k == 1:
                 for copy in soft_copies((0, 1, 2)):
                     copy.wait_recv()
-            else:
-                kv_arrival(k - 1).wait_recv()
-            kv_hop(k).start()
+            kv_copy(k).start()
 
     span = G * length
     factor = math.log2(math.e) / math.sqrt(HD)
@@ -317,7 +308,7 @@
             tile(b, z, True, span)
 
         def earlier_plane(k, _):
-            @pl.when((i == 0) & jnp.logical_not(hops(k + 1)))
+            @pl.when(i == 0)
             def _():
                 kv_arrival(k).wait_recv()
 
@@ -376,8 +367,8 @@
 
     for copy in exchange():
         copy.start()
-    if planes > 2:
-        kv_pass(2)
+    for k in range(2, planes):
+        kv_pass(k)
     for copy in exchange():
         copy.wait_recv()
     square, inner = ex_own[0], ex_own[1]
@@ -401,8 +392,6 @@
     for c in range(hq):
         turn(chunk_heads(c))
         scan_start(1, c)
-    for k in range(3, planes):
-        kv_pass(k)
 
     def intra_backward(hs):
         qs = [lq[:, lanes(h)] for h in hs]
@@ -421,8 +410,12 @@
             gv_acc[:, lanes(h)] = c
 
     for c in range(hq):
+        if c % 2 == 0:
+            intra_backward(chunk_heads(c // 2))
+        scan_middle(1, c)
+    rest = list(range((hq + 1) // 2, hq))
+    for c in rest[:1]:
         intra_backward(chunk_heads(c))
-        scan_middle(1, c)
 
     for copy in soft_copies((3,)):
         copy.wait_recv()
@@ -432,10 +425,12 @@
         for copy in soft_copies((0, 1, 2)):
             copy.wait_recv()
 
-    ahead = jnp.where(z < planes // 2, G, jnp.where(last, 0, 1))
+    ahead = jnp.where(z == 0, G, jnp.where(z < planes // 2, G // 2, 0))
     lax.fori_loop(0, ahead, query_block, 0)
     for c in range(hq):
         scan_end(1, c)
+    for c in rest[1:]:
+        intra_backward(chunk_heads(c))
     lax.fori_loop(ahead, G, query_block, 0)
     soft_out[:, pl.ds(pl.multiple_of(p * qw, HD), qw)] = o_own[p]
 
@@ -464,9 +459,9 @@
         copy.wait_send()
     for k in range(1, planes):
 
-        @pl.when(hops(k))
-        def _():
-            kv_hop(k).wait_send()
+        @pl.when(z + k < planes)
+        def _():
+            kv_copy(k).wait_send()
 
     for way in (0, 1):
 

time: 52.2 us -> 53.2 us (1.019)
  Pallas kernels: 51.4 us -> 52 us
    pallas_call x1, Pallas kernels: 49.9 us -> 50.5 us  [on_device(): pl.pallas_call(functools.partial(kernel, n, n_tp), out_shape=[pltpu.VMEM(...]
where the time goes in v6:
time: 53.2 us; the launch traced here: 52.6 us
  Pallas kernels  52 us (98%)
  between operations  0.64 us (1%)
    pallas_call x1, Pallas kernels, on_device(): pl.pallas_call(functools.partial(kernel, n, n_tp), out_shape=[pltpu.VMEM(...  50.5 us
    pallas_call x1, Pallas kernels, on_device(): pl.pallas_call(write_out, out_shape=[jax.ShapeDtypeStruct((length, w), bf...  1.53 us

profile of v6, /device:TPU:0, one launch (start us, length us, event | category | flops | bytes accessed | tf_op | source)
XLA Modules:
  0.0 52.6 jit_solution(14134595893879763151)
XLA Ops:
  0.6 50.5 %shard_map.119 = (bf16[128,2048]{1,0:T(8,128)(2,1)S(1)}, bf16[128,2048]{1,0:T(8,128)(2,1)S(1)}, bf16[128,2048]{1,0:T(8,128)(2,1)S(1)}, bf16[128,2048]{1,0:T(8,128)(2,1)S(1)}, bf16[128,2048]{1,0:T(8,128)(2,1)S(1)}) custom-call(bf16[128,2048]{1,0:T(8,128)(2,1)} %lq_hbm.1, bf16[128,2048]{1,0:T(8,128)(2,1)} %lk_hbm.1, bf16[128,2048]{1,0:T(8,128)(2,1)} %lv_hbm.1, ...), custom_call_target="tpu_custom_call" | custom-call | tf_op jit(solution)/shard_map/pallas_call | solution.py:527
  51.1 1.5 %shard_map.120 = (bf16[128,2048]{1,0:T(8,128)(2,1)}, bf16[128,2048]{1,0:T(8,128)(2,1)}, bf16[128,2048]{1,0:T(8,128)(2,1)}, bf16[128,2048]{1,0:T(8,128)(2,1)}, bf16[128,2048]{1,0:T(8,128)(2,1)}) custom-call(bf16[128,2048]{1,0:T(8,128)(2,1)S(1)} %get-tuple-element.10.refs_0_, bf16[128,2048]{1,0:T(8,128)(2,1)S(1)} %get-tuple-element.11.refs_1_, ...), custom_call_target="tpu_custom_call" | custom-call | tf_op jit(solution)/shard_map/pallas_call | solution.py:537

commit v7 on v4

--- a/solution.py
+++ b/solution.py
@@ -235,14 +235,8 @@
             scores[h] = w
             mix[:, lanes(h)] = m
 
-    last = z == planes - 1
-
-    def soft_start(which):
-        for copy in soft_copies(which):
-            copy.start()
-
-    pl.when(last)(lambda: soft_start((3,)))
-    pl.when(jnp.logical_not(last))(lambda: soft_start((0, 1, 2)))
+    for copy in soft_copies((0, 1, 2)):
+        copy.start()
     for c in range(hq):
         intra_forward(chunk_heads(c))
 
@@ -260,10 +254,7 @@
     def kv_pass(k):
         @pl.when(hops(k))
         def _():
-            if k == 1:
-                for copy in soft_copies((0, 1, 2)):
-                    copy.wait_recv()
-            else:
+            if k > 1:
                 kv_arrival(k - 1).wait_recv()
             kv_hop(k).start()
 
@@ -340,8 +331,10 @@
     for c in range(hq):
         scan_middle(0, c)
         scan_end(0, c)
-    pl.when(last)(lambda: soft_start((0, 1, 2)))
-    pl.when(jnp.logical_not(last))(lambda: soft_start((3,)))
+    for copy in soft_copies((3,)):
+        copy.start()
+    for copy in soft_copies((0, 1, 2)):
+        copy.wait_recv()
     kv_pass(1)
     loads[6].wait()
 
@@ -426,13 +419,7 @@
 
     for copy in soft_copies((3,)):
         copy.wait_recv()
-
-    @pl.when(last)
-    def _():
-        for copy in soft_copies((0, 1, 2)):
-            copy.wait_recv()
-
-    ahead = jnp.where(z < planes // 2, G, jnp.where(last, 0, 1))
+    ahead = jnp.where(z == 0, G, jnp.where(z < planes // 2, G // 2, 0))
     lax.fori_loop(0, ahead, query_block, 0)
     for c in range(hq):
         scan_end(1, c)

time: 52.2 us -> 51.3 us (0.983)
  Pallas kernels: 51.4 us -> 50.5 us
    pallas_call x1, Pallas kernels: 49.9 us -> 49 us  [on_device(): pl.pallas_call(functools.partial(kernel, n, n_tp), out_shape=[pltpu.VMEM(...]
where the time goes in v7:
time: 51.3 us; the launch traced here: 51.2 us
  Pallas kernels  50.5 us (98%)
  between operations  0.64 us (1%)
    pallas_call x1, Pallas kernels, on_device(): pl.pallas_call(functools.partial(kernel, n, n_tp), out_shape=[pltpu.VMEM(...  49 us
    pallas_call x1, Pallas kernels, on_device(): pl.pallas_call(write_out, out_shape=[jax.ShapeDtypeStruct((length, w), bf...  1.53 us

profile of v7, /device:TPU:0, one launch (start us, length us, event | category | flops | bytes accessed | tf_op | source)
XLA Modules:
  0.0 51.2 jit_solution(17141270958222385326)
XLA Ops:
  0.6 49.0 %shard_map.119 = (bf16[128,2048]{1,0:T(8,128)(2,1)S(1)}, bf16[128,2048]{1,0:T(8,128)(2,1)S(1)}, bf16[128,2048]{1,0:T(8,128)(2,1)S(1)}, bf16[128,2048]{1,0:T(8,128)(2,1)S(1)}, bf16[128,2048]{1,0:T(8,128)(2,1)S(1)}) custom-call(bf16[128,2048]{1,0:T(8,128)(2,1)} %lq_hbm.1, bf16[128,2048]{1,0:T(8,128)(2,1)} %lk_hbm.1, bf16[128,2048]{1,0:T(8,128)(2,1)} %lv_hbm.1, ...), custom_call_target="tpu_custom_call" | custom-call | tf_op jit(solution)/shard_map/pallas_call | solution.py:519
  49.6 1.5 %shard_map.120 = (bf16[128,2048]{1,0:T(8,128)(2,1)}, bf16[128,2048]{1,0:T(8,128)(2,1)}, bf16[128,2048]{1,0:T(8,128)(2,1)}, bf16[128,2048]{1,0:T(8,128)(2,1)}, bf16[128,2048]{1,0:T(8,128)(2,1)}) custom-call(bf16[128,2048]{1,0:T(8,128)(2,1)S(1)} %get-tuple-element.10.refs_0_, bf16[128,2048]{1,0:T(8,128)(2,1)S(1)} %get-tuple-element.11.refs_1_, ...), custom_call_target="tpu_custom_call" | custom-call | tf_op jit(solution)/shard_map/pallas_call | solution.py:529
